TPU v7x, 128 devices: a whole 4x4x4 slice. The times are simulated.
128 devices in a mesh: gauss: 16 (over y, z), view: 8 (over x, core).
Axes of the slice: x: 4, y: 4, z: 4, core: 2. Of those that a mesh axis runs over, the one named last changes fastest.
Arguments:
- table: bfloat16 [262144, 64], P(('gauss', 'view'))
- view_proj: float32 [8, 2, 4], P('view'), may hold values from -3 to 3
- lengths: int32 [8, 256], P('view', 'gauss'), may hold values from 1 to 1024, as said below
- lists: int32 [8, 256, 1024], P('view', 'gauss'), may hold values from 0 to 8191
- requests: int32 [8, 16, 128, 64], P('view', 'gauss'), may hold values from 0 to 2047
- target: bfloat16 [8, 256, 57, 256], P('view', 'gauss'), may hold values from -4 to 4
Outputs:
- image: float32 [8, 256, 57, 256], P('view', 'gauss')
- table_grad: float32 [262144, 64], P(('gauss', 'view'))
Inputs may be any that keep to these rules, and one draw needn't show every extreme that they name: `lengths`: some tile of every view has all 1024 entries live.
All inputs are finite; a program needn't handle non-finite values.
Results may differ from a plain program's by a relative error of at most 0.0003.
Values may be sent and summed in bfloat16 or wider, within the bound.
No kernel may reach another device: no remote copies, remote signals or barrier semaphores. Data moves between devices by JAX's collectives and lax.ppermute only.
A program may use at most 64 MiB of HBM per device.

v0:
```python
import jax
import jax.numpy as jnp
from jax import lax
from jax.sharding import PartitionSpec as P


def splat_block(splats, valid_mask, transmit, camera):
    pixel = jnp.arange(256, dtype=jnp.int32)
    pixel_x = (pixel % 16).astype(jnp.float32) + 0.5
    pixel_y = (pixel // 16).astype(jnp.float32) + 0.5
    proj_u = (
        splats[:, 0] * camera[0, 0]
        + splats[:, 1] * camera[0, 1]
        + splats[:, 2] * camera[0, 2]
        + camera[0, 3]
    )
    proj_w = (
        splats[:, 0] * camera[1, 0]
        + splats[:, 1] * camera[1, 1]
        + splats[:, 2] * camera[1, 2]
        + camera[1, 3]
    )
    center_u = 8.0 + 6.0 * jnp.tanh(proj_u)
    center_w = 8.0 + 6.0 * jnp.tanh(proj_w)
    coef_a = jnp.exp(splats[:, 3])
    coef_c = jnp.exp(splats[:, 4])
    coef_b = 0.9 * jnp.tanh(splats[:, 5]) * jnp.sqrt(coef_a * coef_c)
    opacity = jax.nn.sigmoid(splats[:, 6]) * valid_mask
    delta_u = pixel_x[:, None] - center_u[None, :]
    delta_w = pixel_y[:, None] - center_w[None, :]
    quad = (
        coef_a[None, :] * delta_u * delta_u
        + 2.0 * coef_b[None, :] * delta_u * delta_w
        + coef_c[None, :] * delta_w * delta_w
    )
    alpha = opacity[None, :] * jnp.exp(-0.5 * quad)
    logs = jnp.log1p(-alpha)
    inclusive = jnp.cumsum(logs, axis=1)
    weight = transmit[:, None] * jnp.exp(inclusive - logs) * alpha
    contrib = jnp.dot(
        splats[:, 7:].T,
        weight.T,
        precision=lax.Precision.HIGHEST,
        preferred_element_type=jnp.float32,
    )
    return (contrib, transmit * jnp.exp(inclusive[:, -1]))


def shards(table, view_proj, lengths, lists, requests, target):
    wanted = requests[0, 0]
    peers = wanted.shape[0]
    slots = wanted.shape[1]
    width = table.shape[1]
    incoming = lax.all_to_all(wanted, ("gauss", "view"), split_axis=0, concat_axis=0, tiled=True)
    served = table[incoming]
    fetched = lax.all_to_all(served, ("gauss", "view"), split_axis=0, concat_axis=0, tiled=True)
    fetched = fetched.reshape(peers * slots, width)
    camera = view_proj[0]
    tiles = lists.shape[1]
    entries = lists.shape[2]
    blocks = entries // 256
    channels = width - 7

    def one_tile(tile_index, carry):
        pictures, grads = carry
        ids = lists[0, tile_index]
        splats = fetched[ids].astype(jnp.float32)
        extent = lengths[0, tile_index]
        entry = jnp.arange(entries, dtype=jnp.int32)
        valid_mask = (entry < extent).astype(jnp.float32)

        def forward(block_index, state):
            picture, transmit, starts = state
            lower = block_index * 256
            segment = lax.dynamic_slice_in_dim(splats, lower, 256, 0)
            live = lax.dynamic_slice_in_dim(valid_mask, lower, 256, 0)
            contrib, after = splat_block(segment, live, transmit, camera)
            starts = lax.dynamic_update_index_in_dim(starts, transmit, block_index, 0)
            return (picture + contrib, after, starts)

        begin = (
            jnp.zeros((channels, 256), jnp.float32),
            jnp.ones((256,), jnp.float32),
            jnp.zeros((blocks, 256), jnp.float32),
        )
        picture, unused_final, starts = lax.fori_loop(0, blocks, forward, begin)
        pull_picture = picture - target[0, tile_index].astype(jnp.float32)

        def backward(step_index, state):
            pull_transmit, grow = state
            block_index = blocks - 1 - step_index
            lower = block_index * 256
            segment = lax.dynamic_slice_in_dim(splats, lower, 256, 0)
            live = lax.dynamic_slice_in_dim(valid_mask, lower, 256, 0)
            transmit = lax.dynamic_index_in_dim(starts, block_index, 0, keepdims=False)
            unused_out, pull = jax.vjp(
                lambda values, entering: splat_block(values, live, entering, camera),
                segment,
                transmit,
            )
            grow_block, pull_entering = pull((pull_picture, pull_transmit))
            grow = lax.dynamic_update_slice_in_dim(grow, grow_block, lower, 0)
            return (pull_entering, grow)

        unused_pull, grow = lax.fori_loop(
            0, blocks, backward, (jnp.zeros((256,), jnp.float32), jnp.zeros_like(splats))
        )
        grads = grads.at[ids].add(grow)
        pictures = lax.dynamic_update_index_in_dim(pictures, picture, tile_index, 0)
        return (pictures, grads)

    start_state = (
        jnp.zeros((tiles, channels, 256), jnp.float32),
        jnp.zeros((peers * slots, width), jnp.float32),
    )
    pictures, grads = lax.fori_loop(0, tiles, one_tile, start_state)
    outgoing = grads.reshape(peers, slots, width)
    returned = lax.all_to_all(outgoing, ("gauss", "view"), split_axis=0, concat_axis=0, tiled=True)
    owned = jnp.zeros((table.shape[0], width), jnp.float32)
    owned = owned.at[incoming.reshape(-1)].add(returned.reshape(peers * slots, width))
    return (pictures[None], owned)


def solution(mesh):
    return jax.shard_map(
        shards,
        mesh=mesh,
        in_specs=(
            P(("gauss", "view"), None),
            P("view", None, None),
            P("view", "gauss"),
            P("view", "gauss", None),
            P("view", "gauss", None, None),
            P("view", "gauss", None, None),
        ),
        out_specs=(P("view", "gauss", None, None), P(("gauss", "view"), None)),
        check_vma=False,
    )
```

profile of v0, /device:TPU:1, one launch (start us, length us, event | category | flops | bytes accessed | tf_op | source)
XLA Modules:
  0.0 2206.3 jit_solution(16344481736097655843)
XLA Ops:
  2.1 11.5 all-to-all-start
  23.1 29.3 %gather_fusion.1 = bf16[8192,64]{1,0:T(8,128)(2,1)} fusion(bf16[2048,64]{1,0:T(8,128)(2,1)S(1)} %copy.100, s32[8192]{0:T(1024)S(1)} %broadcast_clamp_fusion.1), kind=kCustom, calls=%fused_computation.1 | custom fusion | bytes 2129920 | tf_op jit(solution)/shard_map/gather | solution.py:55
  62.7 18.4 all-to-all-done.1
  84.6 2011.9 %while.103 = (s32[]{:T(128)}, f32[16,57,256]{2,0,1:T(8,128)}, f32[8192,64]{1,0:T(8,128)}, s32[1,16,1024]{2,1,0:T(8,128)}, bf16[8192,64]{1,0:T(8,128)(2,1)S(1)}, ...) while((s32[]{:T(128)}, f32[16,57,256]{2,0,1:T(8,128)}, ...), condition=%wide.region_19.20_spmd, body=%wide.region_0.19_spmd.sunk | while | flops 169215264 | bytes 12110391 | solution.py:116
  90.1 33.2 %while.104 = (s32[]{:T(128)}, f32[57,256]{1,0:T(8,128)S(1)}, f32[256]{0:T(256)S(1)}, f32[4,256]{1,0:T(4,128)S(1)}, f32[1024,64]{0,1:T(8,128)S(1)}, /*index=5*/f3...) while((s32[]{:T(128)}, f32[57,256]{1,0:T(8,128)S(1)}, ...), condition=%wide.region_4.4_spmd.clone, body=%wide.region_1.3_spmd.clone.sunk | while | flops 55157260 | bytes 1859026 | solution.py:86
  124.1 74.1 %while.105 = (s32[]{:T(128)}, f32[256]{0:T(256)S(1)}, f32[1024,64]{0,1:T(8,128)S(1)}, f32[1024,64]{0,1:T(8,128)S(1)}, f32[1024]{0:T(1024)S(1)}, /*index=5*/f32[2...) while((s32[]{:T(128)}, f32[256]{0:T(256)S(1)}, ...), condition=%wide.region_17.17_spmd.clone, body=%wide.region_5.16_spmd.clone.sunk | while | flops 113957136 | bytes 7614076 | solution.py:105
  215.8 33.2 %while.104 = (s32[]{:T(128)}, f32[57,256]{1,0:T(8,128)S(1)}, f32[256]{0:T(256)S(1)}, f32[4,256]{1,0:T(4,128)S(1)}, f32[1024,64]{0,1:T(8,128)S(1)}, /*index=5*/f3...) while((s32[]{:T(128)}, f32[57,256]{1,0:T(8,128)S(1)}, ...), condition=%wide.region_4.4_spmd.clone, body=%wide.region_1.3_spmd.clone.sunk | while | flops 55157260 | bytes 1859026 | solution.py:86
  249.9 74.1 %while.105 = (s32[]{:T(128)}, f32[256]{0:T(256)S(1)}, f32[1024,64]{0,1:T(8,128)S(1)}, f32[1024,64]{0,1:T(8,128)S(1)}, f32[1024]{0:T(1024)S(1)}, /*index=5*/f32[2...) while((s32[]{:T(128)}, f32[256]{0:T(256)S(1)}, ...), condition=%wide.region_17.17_spmd.clone, body=%wide.region_5.16_spmd.clone.sunk | while | flops 113957136 | bytes 7614076 | solution.py:105
  326.6 9.5 scatter_fusion
  341.6 33.2 %while.104 = (s32[]{:T(128)}, f32[57,256]{1,0:T(8,128)S(1)}, f32[256]{0:T(256)S(1)}, f32[4,256]{1,0:T(4,128)S(1)}, f32[1024,64]{0,1:T(8,128)S(1)}, /*index=5*/f3...) while((s32[]{:T(128)}, f32[57,256]{1,0:T(8,128)S(1)}, ...), condition=%wide.region_4.4_spmd.clone, body=%wide.region_1.3_spmd.clone.sunk | while | flops 55157260 | bytes 1859026 | solution.py:86
  375.6 74.1 %while.105 = (s32[]{:T(128)}, f32[256]{0:T(256)S(1)}, f32[1024,64]{0,1:T(8,128)S(1)}, f32[1024,64]{0,1:T(8,128)S(1)}, f32[1024]{0:T(1024)S(1)}, /*index=5*/f32[2...) while((s32[]{:T(128)}, f32[256]{0:T(256)S(1)}, ...), condition=%wide.region_17.17_spmd.clone, body=%wide.region_5.16_spmd.clone.sunk | while | flops 113957136 | bytes 7614076 | solution.py:105
  452.3 9.5 scatter_fusion
  467.3 33.2 %while.104 = (s32[]{:T(128)}, f32[57,256]{1,0:T(8,128)S(1)}, f32[256]{0:T(256)S(1)}, f32[4,256]{1,0:T(4,128)S(1)}, f32[1024,64]{0,1:T(8,128)S(1)}, /*index=5*/f3...) while((s32[]{:T(128)}, f32[57,256]{1,0:T(8,128)S(1)}, ...), condition=%wide.region_4.4_spmd.clone, body=%wide.region_1.3_spmd.clone.sunk | while | flops 55157260 | bytes 1859026 | solution.py:86
  501.4 74.1 %while.105 = (s32[]{:T(128)}, f32[256]{0:T(256)S(1)}, f32[1024,64]{0,1:T(8,128)S(1)}, f32[1024,64]{0,1:T(8,128)S(1)}, f32[1024]{0:T(1024)S(1)}, /*index=5*/f32[2...) while((s32[]{:T(128)}, f32[256]{0:T(256)S(1)}, ...), condition=%wide.region_17.17_spmd.clone, body=%wide.region_5.16_spmd.clone.sunk | while | flops 113957136 | bytes 7614076 | solution.py:105
  578.1 9.5 scatter_fusion
  593.1 33.2 %while.104 = (s32[]{:T(128)}, f32[57,256]{1,0:T(8,128)S(1)}, f32[256]{0:T(256)S(1)}, f32[4,256]{1,0:T(4,128)S(1)}, f32[1024,64]{0,1:T(8,128)S(1)}, /*index=5*/f3...) while((s32[]{:T(128)}, f32[57,256]{1,0:T(8,128)S(1)}, ...), condition=%wide.region_4.4_spmd.clone, body=%wide.region_1.3_spmd.clone.sunk | while | flops 55157260 | bytes 1859026 | solution.py:86
  627.1 74.1 %while.105 = (s32[]{:T(128)}, f32[256]{0:T(256)S(1)}, f32[1024,64]{0,1:T(8,128)S(1)}, f32[1024,64]{0,1:T(8,128)S(1)}, f32[1024]{0:T(1024)S(1)}, /*index=5*/f32[2...) while((s32[]{:T(128)}, f32[256]{0:T(256)S(1)}, ...), condition=%wide.region_17.17_spmd.clone, body=%wide.region_5.16_spmd.clone.sunk | while | flops 113957136 | bytes 7614076 | solution.py:105
  703.8 9.5 scatter_fusion
  718.8 33.2 %while.104 = (s32[]{:T(128)}, f32[57,256]{1,0:T(8,128)S(1)}, f32[256]{0:T(256)S(1)}, f32[4,256]{1,0:T(4,128)S(1)}, f32[1024,64]{0,1:T(8,128)S(1)}, /*index=5*/f3...) while((s32[]{:T(128)}, f32[57,256]{1,0:T(8,128)S(1)}, ...), condition=%wide.region_4.4_spmd.clone, body=%wide.region_1.3_spmd.clone.sunk | while | flops 55157260 | bytes 1859026 | solution.py:86
  752.8 74.1 %while.105 = (s32[]{:T(128)}, f32[256]{0:T(256)S(1)}, f32[1024,64]{0,1:T(8,128)S(1)}, f32[1024,64]{0,1:T(8,128)S(1)}, f32[1024]{0:T(1024)S(1)}, /*index=5*/f32[2...) while((s32[]{:T(128)}, f32[256]{0:T(256)S(1)}, ...), condition=%wide.region_17.17_spmd.clone, body=%wide.region_5.16_spmd.clone.sunk | while | flops 113957136 | bytes 7614076 | solution.py:105
  829.6 9.5 scatter_fusion
  844.5 33.2 %while.104 = (s32[]{:T(128)}, f32[57,256]{1,0:T(8,128)S(1)}, f32[256]{0:T(256)S(1)}, f32[4,256]{1,0:T(4,128)S(1)}, f32[1024,64]{0,1:T(8,128)S(1)}, /*index=5*/f3...) while((s32[]{:T(128)}, f32[57,256]{1,0:T(8,128)S(1)}, ...), condition=%wide.region_4.4_spmd.clone, body=%wide.region_1.3_spmd.clone.sunk | while | flops 55157260 | bytes 1859026 | solution.py:86
  878.6 74.1 %while.105 = (s32[]{:T(128)}, f32[256]{0:T(256)S(1)}, f32[1024,64]{0,1:T(8,128)S(1)}, f32[1024,64]{0,1:T(8,128)S(1)}, f32[1024]{0:T(1024)S(1)}, /*index=5*/f32[2...) while((s32[]{:T(128)}, f32[256]{0:T(256)S(1)}, ...), condition=%wide.region_17.17_spmd.clone, body=%wide.region_5.16_spmd.clone.sunk | while | flops 113957136 | bytes 7614076 | solution.py:105
  955.3 9.5 scatter_fusion
  970.3 33.2 %while.104 = (s32[]{:T(128)}, f32[57,256]{1,0:T(8,128)S(1)}, f32[256]{0:T(256)S(1)}, f32[4,256]{1,0:T(4,128)S(1)}, f32[1024,64]{0,1:T(8,128)S(1)}, /*index=5*/f3...) while((s32[]{:T(128)}, f32[57,256]{1,0:T(8,128)S(1)}, ...), condition=%wide.region_4.4_spmd.clone, body=%wide.region_1.3_spmd.clone.sunk | while | flops 55157260 | bytes 1859026 | solution.py:86
  1004.3 74.1 %while.105 = (s32[]{:T(128)}, f32[256]{0:T(256)S(1)}, f32[1024,64]{0,1:T(8,128)S(1)}, f32[1024,64]{0,1:T(8,128)S(1)}, f32[1024]{0:T(1024)S(1)}, /*index=5*/f32[2...) while((s32[]{:T(128)}, f32[256]{0:T(256)S(1)}, ...), condition=%wide.region_17.17_spmd.clone, body=%wide.region_5.16_spmd.clone.sunk | while | flops 113957136 | bytes 7614076 | solution.py:105
  1096.0 33.2 %while.104 = (s32[]{:T(128)}, f32[57,256]{1,0:T(8,128)S(1)}, f32[256]{0:T(256)S(1)}, f32[4,256]{1,0:T(4,128)S(1)}, f32[1024,64]{0,1:T(8,128)S(1)}, /*index=5*/f3...) while((s32[]{:T(128)}, f32[57,256]{1,0:T(8,128)S(1)}, ...), condition=%wide.region_4.4_spmd.clone, body=%wide.region_1.3_spmd.clone.sunk | while | flops 55157260 | bytes 1859026 | solution.py:86
  1130.1 74.1 %while.105 = (s32[]{:T(128)}, f32[256]{0:T(256)S(1)}, f32[1024,64]{0,1:T(8,128)S(1)}, f32[1024,64]{0,1:T(8,128)S(1)}, f32[1024]{0:T(1024)S(1)}, /*index=5*/f32[2...) while((s32[]{:T(128)}, f32[256]{0:T(256)S(1)}, ...), condition=%wide.region_17.17_spmd.clone, body=%wide.region_5.16_spmd.clone.sunk | while | flops 113957136 | bytes 7614076 | solution.py:105
  1206.8 9.5 scatter_fusion
  1221.8 33.2 %while.104 = (s32[]{:T(128)}, f32[57,256]{1,0:T(8,128)S(1)}, f32[256]{0:T(256)S(1)}, f32[4,256]{1,0:T(4,128)S(1)}, f32[1024,64]{0,1:T(8,128)S(1)}, /*index=5*/f3...) while((s32[]{:T(128)}, f32[57,256]{1,0:T(8,128)S(1)}, ...), condition=%wide.region_4.4_spmd.clone, body=%wide.region_1.3_spmd.clone.sunk | while | flops 55157260 | bytes 1859026 | solution.py:86
  1255.8 74.1 %while.105 = (s32[]{:T(128)}, f32[256]{0:T(256)S(1)}, f32[1024,64]{0,1:T(8,128)S(1)}, f32[1024,64]{0,1:T(8,128)S(1)}, f32[1024]{0:T(1024)S(1)}, /*index=5*/f32[2...) while((s32[]{:T(128)}, f32[256]{0:T(256)S(1)}, ...), condition=%wide.region_17.17_spmd.clone, body=%wide.region_5.16_spmd.clone.sunk | while | flops 113957136 | bytes 7614076 | solution.py:105
  1347.5 33.2 %while.104 = (s32[]{:T(128)}, f32[57,256]{1,0:T(8,128)S(1)}, f32[256]{0:T(256)S(1)}, f32[4,256]{1,0:T(4,128)S(1)}, f32[1024,64]{0,1:T(8,128)S(1)}, /*index=5*/f3...) while((s32[]{:T(128)}, f32[57,256]{1,0:T(8,128)S(1)}, ...), condition=%wide.region_4.4_spmd.clone, body=%wide.region_1.3_spmd.clone.sunk | while | flops 55157260 | bytes 1859026 | solution.py:86
  1381.6 74.1 %while.105 = (s32[]{:T(128)}, f32[256]{0:T(256)S(1)}, f32[1024,64]{0,1:T(8,128)S(1)}, f32[1024,64]{0,1:T(8,128)S(1)}, f32[1024]{0:T(1024)S(1)}, /*index=5*/f32[2...) while((s32[]{:T(128)}, f32[256]{0:T(256)S(1)}, ...), condition=%wide.region_17.17_spmd.clone, body=%wide.region_5.16_spmd.clone.sunk | while | flops 113957136 | bytes 7614076 | solution.py:105
  1458.3 9.5 scatter_fusion
  1473.3 33.2 %while.104 = (s32[]{:T(128)}, f32[57,256]{1,0:T(8,128)S(1)}, f32[256]{0:T(256)S(1)}, f32[4,256]{1,0:T(4,128)S(1)}, f32[1024,64]{0,1:T(8,128)S(1)}, /*index=5*/f3...) while((s32[]{:T(128)}, f32[57,256]{1,0:T(8,128)S(1)}, ...), condition=%wide.region_4.4_spmd.clone, body=%wide.region_1.3_spmd.clone.sunk | while | flops 55157260 | bytes 1859026 | solution.py:86
  1507.3 74.1 %while.105 = (s32[]{:T(128)}, f32[256]{0:T(256)S(1)}, f32[1024,64]{0,1:T(8,128)S(1)}, f32[1024,64]{0,1:T(8,128)S(1)}, f32[1024]{0:T(1024)S(1)}, /*index=5*/f32[2...) while((s32[]{:T(128)}, f32[256]{0:T(256)S(1)}, ...), condition=%wide.region_17.17_spmd.clone, body=%wide.region_5.16_spmd.clone.sunk | while | flops 113957136 | bytes 7614076 | solution.py:105
  1599.0 33.2 %while.104 = (s32[]{:T(128)}, f32[57,256]{1,0:T(8,128)S(1)}, f32[256]{0:T(256)S(1)}, f32[4,256]{1,0:T(4,128)S(1)}, f32[1024,64]{0,1:T(8,128)S(1)}, /*index=5*/f3...) while((s32[]{:T(128)}, f32[57,256]{1,0:T(8,128)S(1)}, ...), condition=%wide.region_4.4_spmd.clone, body=%wide.region_1.3_spmd.clone.sunk | while | flops 55157260 | bytes 1859026 | solution.py:86
  1633.1 74.1 %while.105 = (s32[]{:T(128)}, f32[256]{0:T(256)S(1)}, f32[1024,64]{0,1:T(8,128)S(1)}, f32[1024,64]{0,1:T(8,128)S(1)}, f32[1024]{0:T(1024)S(1)}, /*index=5*/f32[2...) while((s32[]{:T(128)}, f32[256]{0:T(256)S(1)}, ...), condition=%wide.region_17.17_spmd.clone, body=%wide.region_5.16_spmd.clone.sunk | while | flops 113957136 | bytes 7614076 | solution.py:105
  1709.8 9.5 scatter_fusion
  1724.8 33.2 %while.104 = (s32[]{:T(128)}, f32[57,256]{1,0:T(8,128)S(1)}, f32[256]{0:T(256)S(1)}, f32[4,256]{1,0:T(4,128)S(1)}, f32[1024,64]{0,1:T(8,128)S(1)}, /*index=5*/f3...) while((s32[]{:T(128)}, f32[57,256]{1,0:T(8,128)S(1)}, ...), condition=%wide.region_4.4_spmd.clone, body=%wide.region_1.3_spmd.clone.sunk | while | flops 55157260 | bytes 1859026 | solution.py:86
  1758.8 74.1 %while.105 = (s32[]{:T(128)}, f32[256]{0:T(256)S(1)}, f32[1024,64]{0,1:T(8,128)S(1)}, f32[1024,64]{0,1:T(8,128)S(1)}, f32[1024]{0:T(1024)S(1)}, /*index=5*/f32[2...) while((s32[]{:T(128)}, f32[256]{0:T(256)S(1)}, ...), condition=%wide.region_17.17_spmd.clone, body=%wide.region_5.16_spmd.clone.sunk | while | flops 113957136 | bytes 7614076 | solution.py:105
  1835.5 9.5 scatter_fusion
  1850.5 33.2 %while.104 = (s32[]{:T(128)}, f32[57,256]{1,0:T(8,128)S(1)}, f32[256]{0:T(256)S(1)}, f32[4,256]{1,0:T(4,128)S(1)}, f32[1024,64]{0,1:T(8,128)S(1)}, /*index=5*/f3...) while((s32[]{:T(128)}, f32[57,256]{1,0:T(8,128)S(1)}, ...), condition=%wide.region_4.4_spmd.clone, body=%wide.region_1.3_spmd.clone.sunk | while | flops 55157260 | bytes 1859026 | solution.py:86
  1884.5 74.1 %while.105 = (s32[]{:T(128)}, f32[256]{0:T(256)S(1)}, f32[1024,64]{0,1:T(8,128)S(1)}, f32[1024,64]{0,1:T(8,128)S(1)}, f32[1024]{0:T(1024)S(1)}, /*index=5*/f32[2...) while((s32[]{:T(128)}, f32[256]{0:T(256)S(1)}, ...), condition=%wide.region_17.17_spmd.clone, body=%wide.region_5.16_spmd.clone.sunk | while | flops 113957136 | bytes 7614076 | solution.py:105
  1976.2 33.2 %while.104 = (s32[]{:T(128)}, f32[57,256]{1,0:T(8,128)S(1)}, f32[256]{0:T(256)S(1)}, f32[4,256]{1,0:T(4,128)S(1)}, f32[1024,64]{0,1:T(8,128)S(1)}, /*index=5*/f3...) while((s32[]{:T(128)}, f32[57,256]{1,0:T(8,128)S(1)}, ...), condition=%wide.region_4.4_spmd.clone, body=%wide.region_1.3_spmd.clone.sunk | while | flops 55157260 | bytes 1859026 | solution.py:86
  2010.3 74.1 %while.105 = (s32[]{:T(128)}, f32[256]{0:T(256)S(1)}, f32[1024,64]{0,1:T(8,128)S(1)}, f32[1024,64]{0,1:T(8,128)S(1)}, f32[1024]{0:T(1024)S(1)}, /*index=5*/f32[2...) while((s32[]{:T(128)}, f32[256]{0:T(256)S(1)}, ...), condition=%wide.region_17.17_spmd.clone, body=%wide.region_5.16_spmd.clone.sunk | while | flops 113957136 | bytes 7614076 | solution.py:105
  2113.6 29.2 %all-to-all-done.2 = f32[128,1,4096]{2,1,0:T(1,128)S(1)} async-done(((f32[128,1,4096]{2,1,0:T(1,128)}), f32[128,1,4096]{2,1,0:T(1,128)S(1)}, u32[]{:S(2)}, u32[]{:S(2)}) %all-to-all-start.2) | async-done | bytes 2097184 | tf_op jit(solution)/shard_map/all_to_all | solution.py:118
  2160.6 44.6 %scatter_custom_fusion.1 = f32[2048,64]{1,0:T(8,128)S(1)} fusion(s32[8192]{0:T(1024)S(1)} %bitcast.343, f32[8192,64]{1,0:T(8,128)} %bitcast.324, f32[]{:T(128)} %constant.420.clone.1), kind=kCustom, calls=%fused_computation.215 | custom fusion | flops 524288 | bytes 524800 | tf_op jit(solution)/shard_map/scatter-add | solution.py:120
  (4730 shorter events, 1957.5 us)
Async XLA Ops:
  2.1 20.9 all-to-all-start
  23.0 29.4 %copy-start.4 = (s32[128,1,64]{2,1,0:T(1,128)}, s32[128,1,64]{2,1,0:T(1,128)S(1)}, u32[]{:S(2)}) copy-start(s32[128,1,64]{2,1,0:T(1,128)S(1)} %all-to-all-done) | copy-start | bytes 98308
  52.4 9.4 copy-start.6
  57.1 24.0 %all-to-all-start.1 = ((bf16[128,2,2048]{2,1,0:T(2,128)(2,1)}), bf16[128,2,2048]{2,1,0:T(2,128)(2,1)S(1)}, u32[]{:S(2)}, u32[]{:S(2)}) async-start(bf16[128,2,2048]{2,1,0:T(2,128)(2,1)} %reshape.959), calls=%async_computation.1 | async-start | bytes 2097152 | tf_op jit(solution)/shard_map/all_to_all | solution.py:56
  61.7 22.9 %copy-start = (f32[1,2,4]{2,1,0:T(2,128)S(1)}, f32[1,2,4]{2,1,0:T(2,128)}, u32[]{:S(2)}) copy-start(f32[1,2,4]{2,1,0:T(2,128)} %param.13) | copy-start | bytes 100
  61.7 22.9 %copy-start.7 = (s32[1,16]{1,0:T(1,128)S(1)}, s32[1,16]{1,0:T(1,128)}, u32[]{:S(2)}) copy-start(s32[1,16]{1,0:T(1,128)} %param.14) | copy-start | bytes 196
  142.7 9.2 copy-start.2
  179.7 9.2 copy-start.2
  200.8 9.5 copy-start.8
  305.5 9.2 copy-start.2
  326.6 9.5 copy-start.8
  394.2 9.2 copy-start.2
  431.2 9.2 copy-start.2
  452.3 9.5 copy-start.8
  557.0 9.2 copy-start.2
  578.1 9.5 copy-start.8
  682.7 9.2 copy-start.2
  703.8 9.5 copy-start.8
  771.4 9.2 copy-start.2
  808.5 9.2 copy-start.2
  829.5 9.5 copy-start.8
  897.1 9.2 copy-start.2
  934.2 9.2 copy-start.2
  955.3 9.5 copy-start.8
  1059.9 9.2 copy-start.2
  1081.0 9.5 copy-start.8
  1185.7 9.2 copy-start.2
  1206.8 9.5 copy-start.8
  1274.4 9.2 copy-start.2
  1311.4 9.2 copy-start.2
  1332.5 9.5 copy-start.8
  1400.1 9.2 copy-start.2
  1437.2 9.2 copy-start.2
  1458.3 9.5 copy-start.8
  1525.9 9.2 copy-start.2
  1562.9 9.2 copy-start.2
  1584.0 9.5 copy-start.8
  1651.6 9.2 copy-start.2
  1688.7 9.2 copy-start.2
  1709.8 9.5 copy-start.8
  1814.4 9.2 copy-start.2
  1835.5 9.5 copy-start.8
  1940.2 9.2 copy-start.2
  1961.2 9.5 copy-start.8
  2065.9 9.2 copy-start.2
  2087.0 9.5 copy-start.8
  2102.2 10.5 copy-start.5
  2107.8 35.0 %all-to-all-start.2 = ((f32[128,1,4096]{2,1,0:T(1,128)}), f32[128,1,4096]{2,1,0:T(1,128)S(1)}, u32[]{:S(2)}, u32[]{:S(2)}) async-start(f32[128,1,4096]{2,1,0:T(1,128)} %reshape.961), calls=%async_computation.2 | async-start | bytes 4194304 | tf_op jit(solution)/shard_map/all_to_all | solution.py:118
  (105 other events, 813.3 us)
where the time goes:
time: 2220 us; the launch traced here: 2210 us
  other arithmetic  1530 us (69%)
  local copies, waits for them, and re-layouts  355 us (16%)
  matrix products  229 us (10%)
  waiting for transfers between devices  55.7 us (3%)
    div x128, other arithmetic, splat_block(): opacity = jax.nn.sigmoid(splats[:, 6]) * valid_mask  653 us
    another operation x592, other arithmetic  277 us
    dot_general x192, matrix products, splat_block(): jnp.dot(splats[:, 7:].T, weight.T, precision=lax.Precision.HIGHEST, prefe...  229 us
    scatter-add x16, other arithmetic, one_tile(): grads = grads.at[ids].add(grow)  153 us
    slice x128, local copies, waits for them, and re-layouts, splat_block(): camera[0, 0]  87.1 us
    mul x64, other arithmetic, splat_block(): splats[:, 1] * camera[0, 1]  80.5 us
    mul x64, other arithmetic, splat_block(): splats[:, 1] * camera[1, 1]  80.4 us
    gather x16, local copies, waits for them, and re-layouts, one_tile(): splats = fetched[ids].astype(jnp.float32)  51.3 us

commit v1 on v0

v1 whole, which is shorter than its diff:
```python
import functools

import jax
import jax.numpy as jnp
from jax import lax
from jax.experimental import pallas as pl
from jax.experimental.pallas import tpu as pltpu
from jax.sharding import PartitionSpec as P

LOG2E = 1.4426950408889634
FEATS = 57
ROW = 64
LANE = 128
PIX = 256
GROUP = 32
ACCS = 4
UNROLL = 2
F32 = jnp.float32
BF16 = jnp.bfloat16


def split(x):
    hi = x.astype(BF16)
    lo = (x - hi.astype(F32)).astype(BF16)
    return hi, lo


def dot(a, b):
    return jnp.dot(a, b, preferred_element_type=F32)


def dot_t(a, b):
    return lax.dot_general(a, b, (((1,), (1,)), ((), ())), preferred_element_type=F32)


def unpack_rows(pairs_ref, rows_ref, peers):
    def step(i, c):
        for k in range(8):
            o = i * 8 + k
            two = pairs_ref[pl.ds(pl.multiple_of(o * 32, 32), 32), :].astype(F32)
            base = pl.multiple_of(o * 64, 64)
            rows_ref[pl.ds(base, 32), :] = two
            rows_ref[pl.ds(pl.multiple_of(base + 32, 32), 32), :] = pltpu.roll(two, 64, 1)
        return c

    lax.fori_loop(0, peers // 8, step, 0)


def pack_rows(accs, pairs_ref, peers):
    lane = lax.broadcasted_iota(jnp.int32, (32, LANE), 1)

    def step(i, c):
        for k in range(4):
            o = i * 4 + k
            base = pl.multiple_of(o * 64, 64)
            first = sum(acc[pl.ds(base, 32), :] for acc in accs)
            second = sum(acc[pl.ds(pl.multiple_of(base + 32, 32), 32), :] for acc in accs)
            pairs_ref[pl.ds(pl.multiple_of(o * 32, 32), 32), :] = jnp.where(
                lane < 64, first, pltpu.roll(second, 64, 1)
            )
        return c

    lax.fori_loop(0, peers // 4, step, 0)


def tiles_kernel(
    lens, lists, cam,
    pairs, target, prefix_mat, suffix_mat,
    image, out_pairs,
    rows, acc0, acc1, acc2, acc3, splats, grows, feat_t, par, geo, mom, weights, ratio, pic, tgt, grow_t,
):
    tiles = lens.shape[0]
    peers = pairs.shape[0] // 32
    accs = (acc0, acc1, acc2, acc3)
    entries = splats.shape[0]
    unpack_rows(pairs, rows, peers)

    def clear(i, c):
        for acc in accs:
            acc[pl.ds(pl.multiple_of(i * 64, 64), 64), :] = jnp.zeros((64, LANE), F32)
        return c

    lax.fori_loop(0, acc0.shape[0] // 64, clear, 0)
    tgt[...] = target[...].astype(F32)
    splats[...] = jnp.zeros_like(splats)
    feat_t[...] = jnp.zeros_like(feat_t)
    par[...] = jnp.zeros_like(par)
    mom[...] = jnp.zeros_like(mom)

    prefix = prefix_mat[...]
    suffix = suffix_mat[...]
    sub16 = lax.broadcasted_iota(jnp.int32, (16, LANE), 0).astype(F32) + 0.5

    def one_tile(t, carry):
        extent = lens[t]
        groups = (extent + GROUP - 1) // GROUP
        steps = (extent + UNROLL * LANE - 1) // (UNROLL * LANE)

        def gather(i, c):
            base = pl.multiple_of(i * GROUP, GROUP)
            got = [rows[pl.ds(lists[t * entries + base + j], 1), :] for j in range(GROUP)]
            for j in range(GROUP):
                splats[pl.ds(base + j, 1), :] = got[j]
            return c

        lax.fori_loop(0, groups, gather, 0)

        for b in range(8):
            @pl.when(b * LANE < extent)
            def _():
                turned = jnp.transpose(splats[b * LANE:(b + 1) * LANE, :])
                par[b * 8:(b + 1) * 8, :] = turned[56:64, :]
                feat_t[b] = turned[0:64, :].astype(BF16)

        entry = (
            lax.broadcasted_iota(jnp.int32, (8, LANE), 0) * LANE
            + lax.broadcasted_iota(jnp.int32, (8, LANE), 1)
        )

        def param(j):
            return jnp.where(entry < extent, par[pl.ds(j + 1, 8, stride=8), :], 0.0)

        px, py, pz = param(0), param(1), param(2)
        sa, sc, sb, so = param(3), param(4), param(5), param(6)
        tu = jnp.tanh(px * cam[0, 0] + py * cam[0, 1] + pz * cam[0, 2] + cam[0, 3])
        tw = jnp.tanh(px * cam[1, 0] + py * cam[1, 1] + pz * cam[1, 2] + cam[1, 3])
        ca, cc = jnp.exp(sa), jnp.exp(sc)
        tb = jnp.tanh(sb)
        root = 0.9 * jnp.sqrt(ca * cc)
        cb = tb * root
        soft = jnp.exp(-jnp.abs(so))
        log_o = jnp.minimum(so, 0.0) * LOG2E - jnp.log2(1.0 + soft)
        log_o = jnp.where(entry < extent, log_o, -1e30)
        rest = jnp.where(so >= 0.0, soft, 1.0) / (1.0 + soft)
        half = -0.5 * LOG2E
        geo[0] = 8.0 + 6.0 * tu
        geo[1] = 8.0 + 6.0 * tw
        geo[2] = half * ca
        geo[3] = (2.0 * half) * cb
        geo[4] = half * cc
        geo[5] = log_o

        pic[...] = jnp.zeros((64, PIX), F32)

        def coords(b):
            dx = sub16 - geo[0, pl.ds(b, 1), :]
            dy = sub16 - geo[1, pl.ds(b, 1), :]
            return dx, dy

        def forward(i, entering):
            for k in range(UNROLL):
                b = i * UNROLL + k
                dx, dy = coords(b)
                qa = geo[2, pl.ds(b, 1), :] * dx * dx
                qb = geo[3, pl.ds(b, 1), :] * dx
                qc = geo[4, pl.ds(b, 1), :] * dy * dy + geo[5, pl.ds(b, 1), :]
                power = qa[None] + qb[None] * dy[:, None, :] + qc[:, None, :]
                alpha = jnp.exp2(power.reshape(PIX, LANE))
                logs = jnp.log2(1.0 - alpha)
                ratio[b] = alpha * jnp.exp2(-logs)
                both = dot(jnp.concatenate(split(logs), axis=1), prefix)
                weight = alpha * jnp.exp2(both[:, :LANE] + entering)
                entering = entering + both[:, LANE:]
                halves = jnp.concatenate(split(weight), axis=1)
                weights[b] = halves
                ft = feat_t[b]
                pic[...] += dot_t(jnp.concatenate([ft, ft], axis=1), halves)
            return entering

        lax.fori_loop(0, steps, forward, jnp.zeros((PIX, LANE), F32))

        picture = pic[...]
        for h in range(2):
            image[h, pl.ds(t, FEATS, stride=tiles), :] = picture[:FEATS, h * LANE:(h + 1) * LANE]
        want = jnp.concatenate(
            [tgt[h, pl.ds(t, FEATS, stride=tiles), :] for h in range(2)], axis=1
        )
        want = jnp.concatenate([want, jnp.zeros((64 - FEATS, PIX), F32)], axis=0)
        feature = lax.broadcasted_iota(jnp.int32, (64, PIX), 0) < FEATS
        pull = jnp.where(feature, picture - want, 0.0)
        pull_hi, pull_lo = split(pull)
        pull_rows = jnp.concatenate([pull_hi, pull_lo], axis=0)
        pull_t = jnp.transpose(
            jnp.concatenate([pull_hi.astype(F32), pull_lo.astype(F32)], axis=0)
        ).astype(BF16)

        def backward(i, later):
            for k in range(UNROLL):
                b = (steps - 1 - i) * UNROLL + (UNROLL - 1 - k)
                dx, dy = coords(b)
                ft = feat_t[b]
                d_weight = dot(pull_t, jnp.concatenate([ft, ft], axis=0))
                halves = weights[b]
                weight = halves[:, :LANE].astype(F32) + halves[:, LANE:].astype(F32)
                prod = weight * d_weight
                both = dot(jnp.concatenate(split(prod), axis=1), suffix)
                h = prod - ratio[b] * (both[:, :LANE] + later)
                later = later + both[:, LANE:]
                h = h.reshape(16, 16, LANE)
                hy = h * dy[:, None, :]
                s0 = jnp.sum(h, axis=0)
                s1 = jnp.sum(hy, axis=0)
                s2 = jnp.sum(hy * dy[:, None, :], axis=0)
                sx = s0 * dx
                for j, m in enumerate((s0, sx, s1, sx * dx, s1 * dx, s2)):
                    mom[j, pl.ds(b, 1), :] = jnp.sum(m, axis=0, keepdims=True)
                quads = dot(pull_rows, halves)
                quads = quads[:64] + quads[64:]
                grow_t[b] = quads[:, :LANE] + quads[:, LANE:]
            return later

        lax.fori_loop(0, steps, backward, jnp.zeros((PIX, LANE), F32))

        m0, mx, my, mxx, mxy, myy = (mom[j] for j in range(6))
        du = (ca * mx + cb * my) * 6.0 * (1.0 - tu * tu)
        dw = (cb * mx + cc * my) * 6.0 * (1.0 - tw * tw)
        shared = -0.5 * cb * mxy
        outs = (
            du * cam[0, 0] + dw * cam[1, 0],
            du * cam[0, 1] + dw * cam[1, 1],
            du * cam[0, 2] + dw * cam[1, 2],
            -0.5 * ca * mxx + shared,
            -0.5 * cc * myy + shared,
            -mxy * root * (1.0 - tb * tb),
            rest * m0,
        )
        for j, value in enumerate(outs):
            par[pl.ds(j + 1, 8, stride=8), :] = value
        keep = lax.broadcasted_iota(jnp.int32, (8, LANE), 0) == 0

        for b in range(8):
            @pl.when(b * LANE < extent)
            def _():
                last = jnp.where(keep, grow_t[b, 56:64, :], par[b * 8:(b + 1) * 8, :])
                whole = jnp.concatenate([grow_t[b, 0:56, :], last, jnp.zeros((64, LANE), F32)], axis=0)
                grows[b * LANE:(b + 1) * LANE, :] = jnp.transpose(whole)

        def scatter(i, c):
            base = pl.multiple_of(i * GROUP, GROUP)
            block = [grows[pl.ds(base + j, 1), :] for j in range(GROUP)]
            ids = [lists[t * entries + base + j] for j in range(GROUP)]

            for j in range(0, GROUP, ACCS):
                old = [accs[k][pl.ds(ids[j + k], 1), :] for k in range(ACCS)]
                for k in range(ACCS):
                    accs[k][pl.ds(ids[j + k], 1), :] = old[k] + block[j + k]
            return c

        lax.fori_loop(0, groups, scatter, 0)
        return carry

    lax.fori_loop(0, tiles, one_tile, 0)
    pack_rows(accs, out_pairs, peers)


def triangles():
    r = lax.broadcasted_iota(jnp.int32, (PIX, PIX), 0) % LANE
    c = lax.broadcasted_iota(jnp.int32, (PIX, PIX), 1)
    prefix = (c >= LANE) | (r < c)
    suffix = (c >= LANE) | (r > c)
    return prefix.astype(BF16), suffix.astype(BF16)


def render(lens, lists, cam, pairs, target):
    tiles, entries = lists.shape
    peers = pairs.shape[0] // 32
    smem = pl.BlockSpec(memory_space=pltpu.SMEM)
    vmem = pl.BlockSpec(memory_space=pltpu.VMEM)
    prefix, suffix = triangles()
    t2 = jnp.transpose(target, (1, 0, 2)).reshape(FEATS * tiles, PIX)
    t2 = jnp.stack([t2[:, :LANE], t2[:, LANE:]])
    image, grads = pl.pallas_call(
        tiles_kernel,
        out_shape=(
            jax.ShapeDtypeStruct((2, FEATS * tiles, LANE), F32),
            jax.ShapeDtypeStruct((peers * 32, LANE), F32),
        ),
        in_specs=[smem] * 3 + [vmem] * 4,
        out_specs=(vmem, vmem),
        scratch_shapes=[
            *[pltpu.VMEM((peers * 64, LANE), F32)] * (1 + ACCS),
            pltpu.VMEM((entries, LANE), F32),
            pltpu.VMEM((entries, LANE), F32),
            pltpu.VMEM((8, ROW, LANE), BF16),
            pltpu.VMEM((64, LANE), F32),
            pltpu.VMEM((6, 8, LANE), F32),
            pltpu.VMEM((6, 8, LANE), F32),
            pltpu.VMEM((8, PIX, 2 * LANE), BF16),
            pltpu.VMEM((8, PIX, LANE), F32),
            pltpu.VMEM((64, PIX), F32),
            pltpu.VMEM((2, FEATS * tiles, LANE), F32),
            pltpu.VMEM((8, ROW, LANE), F32),
        ],
        compiler_params=pltpu.CompilerParams(vmem_limit_bytes=48 << 20),
    )(lens, lists.reshape(-1), cam, pairs, t2, prefix, suffix)
    image = jnp.concatenate([image[0], image[1]], axis=1).reshape(FEATS, tiles, PIX)
    return jnp.transpose(image, (1, 0, 2)), grads


def serve_kernel(slot_major, table_lo, served):
    peers = slot_major.shape[1]
    lane = lax.broadcasted_iota(jnp.int32, (64, LANE), 1)
    upper = lane // 64
    mat = table_lo[...]

    def step(g, c):
        ids = pltpu.roll(slot_major[...], lax.rem(peers - g * 8, peers), 1)
        for k in range(8):
            col = jnp.broadcast_to(ids[:, k:k + 1], (64, LANE))
            low = col & 255
            high = (col >> 8) - upper
            hot = [jnp.where(low == lane + q * LANE, 1.0, 0.0).astype(BF16) for q in range(2)]
            got = dot_t(jnp.concatenate(hot, axis=1), mat)
            total = jnp.zeros((64, LANE), F32)
            for q in range(4):
                total = total + jnp.where(high == 2 * q, got[:, q * LANE:(q + 1) * LANE], 0.0)
            total = total + pltpu.roll(total, 64, 1)
            out = jnp.where(lane[:32] < 64, total[:32], total[32:])
            served[pl.ds(pl.multiple_of((g * 8 + k) * 32, 32), 32), :] = out.astype(BF16)
        return c

    lax.fori_loop(0, peers // 8, step, 0)


def serve(incoming, table):
    peers = incoming.shape[0]
    turned = jnp.transpose(table)
    turned = jnp.concatenate([turned[ROW - FEATS:], turned[:ROW - FEATS]], axis=0)
    turned = turned.reshape(ROW, 8, PIX).transpose(1, 0, 2).reshape(8 * ROW, PIX)
    vmem = pl.BlockSpec(memory_space=pltpu.VMEM)
    return pl.pallas_call(
        serve_kernel,
        out_shape=jax.ShapeDtypeStruct((peers * 32, LANE), BF16),
        in_specs=[vmem, vmem],
        out_specs=vmem,
        compiler_params=pltpu.CompilerParams(vmem_limit_bytes=32 << 20),
    )(jnp.transpose(incoming), turned)


def collect_kernel(slot_major, flat, pairs, owned, total):
    peers = slot_major.shape[1]
    lane = lax.broadcasted_iota(jnp.int32, (64, LANE), 1)
    upper = lane // 64
    left = lane[:32] < 64
    low_id = lax.broadcasted_iota(jnp.int32, (512, LANE), 0)
    total[...] = jnp.zeros_like(total)

    def step(g, c):
        ids = pltpu.roll(slot_major[...], lax.rem(peers - g * 8, peers), 1)
        hot = []
        for k in range(4):
            row = flat[pl.ds(g * 4 + k, 1), :] & 511
            hot.append(jnp.where(low_id == row, 1.0, 0.0).astype(BF16))
        blocks = []
        for k in range(8):
            high = (jnp.broadcast_to(ids[:, k:k + 1], (64, LANE)) >> 9) - upper
            two = pairs[pl.ds(pl.multiple_of((g * 8 + k) * 32, 32), 32), :]
            other = pltpu.roll(two, 64, 1)
            both = jnp.concatenate(
                [jnp.where(left, two, other), jnp.where(left, other, two)], axis=0
            )
            hi = both.astype(BF16).astype(F32)
            parts = [
                jnp.where(high == 2 * q, part, 0.0).astype(BF16)
                for part in (hi, both - hi)
                for q in range(2)
            ]
            blocks.append(jnp.concatenate(parts, axis=1))
        total[...] += dot(jnp.concatenate(hot, axis=1), jnp.concatenate(blocks, axis=0))
        return c

    lax.fori_loop(0, peers // 8, step, 0)
    whole = jnp.transpose(total[:, :256] + total[:, 256:])
    for q in range(4):
        part = whole[q * 64:(q + 1) * 64]
        owned[:, q * 512:(q + 1) * 512] = jnp.concatenate([part[FEATS:], part[:FEATS]], axis=0)


def collect(incoming, pairs, rows):
    peers = incoming.shape[0]
    vmem = pl.BlockSpec(memory_space=pltpu.VMEM)
    owned = pl.pallas_call(
        collect_kernel,
        out_shape=jax.ShapeDtypeStruct((ROW, rows), F32),
        in_specs=[vmem] * 3,
        out_specs=vmem,
        scratch_shapes=[pltpu.VMEM((512, 512), F32)],
        compiler_params=pltpu.CompilerParams(vmem_limit_bytes=32 << 20),
    )(jnp.transpose(incoming), incoming.reshape(-1, LANE), pairs)
    return jnp.transpose(owned)


def exchange(x):
    return lax.all_to_all(x, ("gauss", "view"), split_axis=0, concat_axis=0, tiled=True)


def shards(table, view_proj, lengths, lists, requests, target):
    incoming = exchange(requests[0, 0])
    peers = incoming.shape[0]
    served = serve(incoming, table)
    pairs = exchange(served.reshape(peers, 32, LANE)).reshape(peers * 32, LANE)
    image, grads = render(lengths[0], lists[0], view_proj[0], pairs, target[0])
    returned = exchange(grads.reshape(peers, 32, LANE)).reshape(peers * 32, LANE)
    return image[None], collect(incoming, returned, table.shape[0])


def solution(mesh):
    return jax.shard_map(
        shards,
        mesh=mesh,
        in_specs=(
            P(("gauss", "view"), None),
            P("view", None, None),
            P("view", "gauss"),
            P("view", "gauss", None),
            P("view", "gauss", None, None),
            P("view", "gauss", None, None),
        ),
        out_specs=(P("view", "gauss", None, None), P(("gauss", "view"), None)),
        check_vma=False,
    )
```

time: 2220 us -> 225 us (0.10)
  other arithmetic: 1530 us -> 2.07 us
  local copies, waits for them, and re-layouts: 355 us -> 5.39 us
  matrix products: 229 us -> 0 us
  Pallas kernels: 0 us -> 117 us
  starting transfers between devices: 20.5 us -> 49.8 us
    div x128 -> x0, other arithmetic: 653 us -> none  [splat_block(): opacity = jax.nn.sigmoid(splats[:, 6]) * valid_mask]
    mul x1024 -> x0, other arithmetic: 306 us -> none  [the longest x64 80.5 us: splat_block(): splats[:, 1] * camera[0, 1]]
    another operation x592 -> x1, other arithmetic: 277 us -> 0.05 us  [render(): t2 = jnp.stack([t2[:, :LANE], t2[:, LANE:]])]
    dot_general x192 -> x0, matrix products: 229 us -> none  [splat_block(): jnp.dot(splats[:, 7:].T, weight.T, precision=lax.Precision.HIGHEST, prefe...]
    scatter-add x17 -> x0, other arithmetic: 197 us -> none  [the longest x16 153 us: one_tile(): grads = grads.at[ids].add(grow)]
    pallas_call x0 -> x3, Pallas kernels: none -> 117 us  [the longest x1 90.2 us: render(): pl.pallas_call(tiles_kernel, out_shape=(jax.ShapeDtypeStruct((2, FEATS *...]
    slice x128 -> x3, local copies, waits for them, and re-layouts: 87.1 us -> 1.84 us  [the longest x1 1.01 us: serve(): turned[ROW - FEATS:]]
    gather x17 -> x0, local copies, waits for them, and re-layouts: 80.6 us -> none  [the longest x16 51.3 us: one_tile(): splats = fetched[ids].astype(jnp.float32)]
where the time goes in v1:
time: 225 us; the launch traced here: 229 us
  Pallas kernels  117 us (52%)
  waiting for transfers between devices  54.6 us (24%)
  starting transfers between devices  49.8 us (22%)
  local copies, waits for them, and re-layouts  5.39 us (2%)
    pallas_call x1, Pallas kernels, render(): pl.pallas_call(tiles_kernel, out_shape=(jax.ShapeDtypeStruct((2, FEATS *...  90.2 us
    all_to_all x3, waiting for transfers between devices, exchange(): lax.all_to_all(x, ('gauss', 'view'), split_axis=0, concat_axis=0, tiled=T...  54.6 us
    all_to_all x3, starting transfers between devices, exchange(): lax.all_to_all(x, ('gauss', 'view'), split_axis=0, concat_axis=0, tiled=T...  49.8 us
    pallas_call x1, Pallas kernels, serve(): pl.pallas_call(serve_kernel, out_shape=jax.ShapeDtypeStruct((peers * 32,...  15.8 us
    pallas_call x1, Pallas kernels, collect(): pl.pallas_call(collect_kernel, out_shape=jax.ShapeDtypeStruct((ROW, rows)...  10.7 us
  transfers between devices with their start and end apart: 3, of which 3 were waited for; matrix products, arithmetic and copies ran while one was open for 2% of the time, Pallas kernels for 0%

profile of v1, /device:TPU:1, one launch (start us, length us, event | category | flops | bytes accessed | tf_op | source)
XLA Modules:
  0.0 229.3 jit_solution(17054123028571983445)
XLA Ops:
  0.6 1.5 copy.12
  2.1 11.5 %all-to-all-start = ((s32[128,1,64]{2,1,0:T(1,128)}), s32[128,1,64]{2,1,0:T(1,128)S(1)}, u32[]{:S(2)}, u32[]{:S(2)}) async-start(s32[128,1,64]{2,1,0:T(1,128)} %bitcast.2), calls=%async_computation | async-start | bytes 131072 | tf_op jit(solution)/shard_map/all_to_all | solution.py:394
  13.6 0.8 slice.25
  14.4 1.0 slice.24
  15.4 0.0 copy-start.4
  15.4 0.0 copy-start.3
  15.5 7.6 %all-to-all-done = s32[128,1,64]{2,1,0:T(1,128)S(1)} async-done(((s32[128,1,64]{2,1,0:T(1,128)}), s32[128,1,64]{2,1,0:T(1,128)S(1)}, u32[]{:S(2)}, u32[]{:S(2)}) %all-to-all-start) | async-done | bytes 32800 | tf_op jit(solution)/shard_map/all_to_all | solution.py:394
  23.0 0.1 copy.13
  23.1 15.8 %shard_map.77 = bf16[4096,128]{1,0:T(8,128)(2,1)} custom-call(s32[64,128]{1,0:T(8,128)S(1)} %bitcast.40, bf16[512,256]{1,0:T(8,128)(2,1)S(1)} %bitcast.39), custom_call_target="tpu_custom_call" | custom-call | tf_op jit(solution)/shard_map/pallas_call | solution.py:331
  38.9 0.0 copy-start.1
  38.9 0.0 copy-start.2
  39.0 4.6 %all-to-all-start.1 = ((bf16[128,32,128]{2,1,0:T(8,128)(2,1)}), bf16[128,32,128]{2,1,0:T(8,128)(2,1)S(1)}, u32[]{:S(2)}, u32[]{:S(2)}) async-start(bf16[128,32,128]{2,1,0:T(8,128)(2,1)} %bitcast.8), calls=%async_computation.1 | async-start | bytes 2097152 | tf_op jit(solution)/shard_map/all_to_all | solution.py:394
  43.6 0.0 copy-done.4
  43.6 0.0 copy-done.3
  43.7 0.2 fusion.3
  43.9 19.0 %all-to-all-done.1 = bf16[128,32,128]{2,1,0:T(8,128)(2,1)S(1)} async-done(((bf16[128,32,128]{2,1,0:T(8,128)(2,1)}), bf16[128,32,128]{2,1,0:T(8,128)(2,1)S(1)}, u32[]{:S(2)}, u32[]{:S(2)}) %all-to-all-start.1) | async-done | bytes 1048608 | tf_op jit(solution)/shard_map/all_to_all | solution.py:394
  62.9 0.0 copy-done.1
  62.9 0.0 copy-done.2
  62.9 90.2 %shard_map.78 = (f32[2,912,128]{2,1,0:T(8,128)S(1)}, f32[4096,128]{1,0:T(8,128)S(1)}) custom-call(s32[16]{0:T(128)S(1)} %bitcast.44, s32[16384]{0:T(1024)S(1)} %bitcast.42, f32[2,4]{1,0:T(2,128)S(1)} %bitcast.43, bf16[4096,128]{1,0:T(8,128)(2,1)S(1)} %bitcast.37, bf16[2,912,128]{2,1,0:T(8,128)(2,1)S(1)} %pad_maximum_fusion.target, ...), custom_call_target="tpu_custom_call" | custom-call | tf_op jit(solution)/shard_map/pallas_call | solution.py:272
  153.1 0.0 copy-start
  153.1 1.3 copy-done
  154.4 33.7 %all-to-all-start.2 = ((f32[128,32,128]{2,1,0:T(8,128)}), f32[128,32,128]{2,1,0:T(8,128)S(1)}, u32[]{:S(2)}, u32[]{:S(2)}) async-start(f32[128,32,128]{2,1,0:T(8,128)} %bitcast.38), calls=%async_computation.2 | async-start | bytes 4194304 | tf_op jit(solution)/shard_map/all_to_all | solution.py:394
  188.1 0.5 broadcast.25
  188.6 0.8 reduce.3
  189.4 0.1 reshape.42.flat
  189.5 0.1 fusion.5
  189.5 1.0 maximum_bitcast_fusion
  190.5 28.0 %all-to-all-done.2 = f32[128,32,128]{2,1,0:T(8,128)S(1)} async-done(((f32[128,32,128]{2,1,0:T(8,128)}), f32[128,32,128]{2,1,0:T(8,128)S(1)}, u32[]{:S(2)}, u32[]{:S(2)}) %all-to-all-start.2) | async-done | bytes 2097184 | tf_op jit(solution)/shard_map/all_to_all | solution.py:394
  218.6 10.7 %shard_map.79 = f32[64,2048]{1,0:T(8,128)} custom-call(s32[64,128]{1,0:T(8,128)S(1)} %bitcast.41, s32[64,128]{1,0:T(8,128)S(1)} %reshape.42.flat, f32[4096,128]{1,0:T(8,128)S(1)} %bitcast.36), custom_call_target="tpu_custom_call" | custom-call | tf_op jit(solution)/shard_map/pallas_call | solution.py:382
  (7 shorter events, 0.1 us)
Async XLA Ops:
  2.1 20.9 %all-to-all-start = ((s32[128,1,64]{2,1,0:T(1,128)}), s32[128,1,64]{2,1,0:T(1,128)S(1)}, u32[]{:S(2)}, u32[]{:S(2)}) async-start(s32[128,1,64]{2,1,0:T(1,128)} %bitcast.2), calls=%async_computation | async-start | bytes 131072 | tf_op jit(solution)/shard_map/all_to_all | solution.py:394
  15.4 28.1 %copy-start.4 = (s32[1,16,1024]{2,1,0:T(8,128)S(1)}, s32[1,16,1024]{2,1,0:T(8,128)}, u32[]{:S(2)}) copy-start(s32[1,16,1024]{2,1,0:T(8,128)} %param.9) | copy-start | bytes 196612
  15.4 28.2 %copy-start.3 = (bf16[1,16,57,256]{3,1,2,0:T(8,128)(2,1)S(1)}, bf16[1,16,57,256]{3,1,2,0:T(8,128)(2,1)}, u32[]{:S(2)}) copy-start(bf16[1,16,57,256]{3,1,2,0:T(8,128)(2,1)} %param.11) | copy-start | bytes 1400836
  38.9 24.0 %copy-start.1 = (f32[1,2,4]{2,1,0:T(2,128)S(1)}, f32[1,2,4]{2,1,0:T(2,128)}, u32[]{:S(2)}) copy-start(f32[1,2,4]{2,1,0:T(2,128)} %param.7) | copy-start | bytes 100
  38.9 24.0 %copy-start.2 = (s32[1,16]{1,0:T(1,128)S(1)}, s32[1,16]{1,0:T(1,128)}, u32[]{:S(2)}) copy-start(s32[1,16]{1,0:T(1,128)} %param.8) | copy-start | bytes 196
  39.0 24.0 %all-to-all-start.1 = ((bf16[128,32,128]{2,1,0:T(8,128)(2,1)}), bf16[128,32,128]{2,1,0:T(8,128)(2,1)S(1)}, u32[]{:S(2)}, u32[]{:S(2)}) async-start(bf16[128,32,128]{2,1,0:T(8,128)(2,1)} %bitcast.8), calls=%async_computation.1 | async-start | bytes 2097152 | tf_op jit(solution)/shard_map/all_to_all | solution.py:394
  153.1 1.3 copy-start
  154.4 64.2 %all-to-all-start.2 = ((f32[128,32,128]{2,1,0:T(8,128)}), f32[128,32,128]{2,1,0:T(8,128)S(1)}, u32[]{:S(2)}, u32[]{:S(2)}) async-start(f32[128,32,128]{2,1,0:T(8,128)} %bitcast.38), calls=%async_computation.2 | async-start | bytes 4194304 | tf_op jit(solution)/shard_map/all_to_all | solution.py:394

commit v2 on v1

v2 whole, which is shorter than its diff:
```python
import functools

import jax
import jax.numpy as jnp
from jax import lax
from jax.experimental import pallas as pl
from jax.experimental.pallas import tpu as pltpu
from jax.sharding import PartitionSpec as P

LOG2E = 1.4426950408889634
FEATS = 57
ROW = 64
LANE = 128
PIX = 256
ACCS = 4
STEP = 256
RING = 9
PAD = 16
F32 = jnp.float32
BF16 = jnp.bfloat16


def split(x):
    hi = x.astype(BF16)
    lo = (x - hi.astype(F32)).astype(BF16)
    return hi, lo


def dot(a, b):
    return jnp.dot(a, b, preferred_element_type=F32)


def dot_t(a, b):
    return lax.dot_general(a, b, (((1,), (1,)), ((), ())), preferred_element_type=F32)


def unpack_rows(pairs_ref, rows_ref, peers):
    def step(i, c):
        for k in range(8):
            o = i * 8 + k
            two = pairs_ref[pl.ds(pl.multiple_of(o * 32, 32), 32), :].astype(F32)
            base = pl.multiple_of(o * 64, 64)
            rows_ref[pl.ds(base, 32), :] = two
            rows_ref[pl.ds(pl.multiple_of(base + 32, 32), 32), :] = pltpu.roll(two, 64, 1)
        return c

    lax.fori_loop(0, peers // 8, step, 0)


def pack_rows(accs, pairs_ref, peers):
    lane = lax.broadcasted_iota(jnp.int32, (32, LANE), 1)

    def step(i, c):
        for k in range(4):
            o = i * 4 + k
            base = pl.multiple_of(o * 64, 64)
            first = sum(acc[pl.ds(base, 32), :] for acc in accs)
            second = sum(acc[pl.ds(pl.multiple_of(base + 32, 32), 32), :] for acc in accs)
            pairs_ref[pl.ds(pl.multiple_of(o * 32, 32), 32), :] = jnp.where(
                lane < 64, first, pltpu.roll(second, 64, 1)
            )
        return c

    lax.fori_loop(0, peers // 4, step, 0)


def tiles_kernel(
    lens, lists, cam,
    pairs, target, prefix_mat, suffix_mat,
    image, out_pairs,
    base_of, tile_of, first_of, mirror_of, live_of,
    rows, acc0, acc1, acc2, acc3,
    splats, grows, feat_t, geo, weights, ratio, entering_ref, later_ref, pic, tgt, pull_rows, pull_t, grow_t,
):
    accs = (acc0, acc1, acc2, acc3)
    tiles = lens.shape[0]
    peers = pairs.shape[0] // 32
    entries = lists.shape[0] // (tiles + 1)

    def blank(i, c):
        base_of[i] = tiles * entries
        tile_of[i] = 0
        first_of[i] = 1
        mirror_of[i] = 0
        live_of[i] = 0
        return c

    lax.fori_loop(0, base_of.shape[0], blank, 0)

    def list_tile(t, at):
        steps = (lens[t] + STEP - 1) // STEP

        def list_step(j, c):
            where = at + j + PAD
            base_of[where] = t * entries + j * STEP
            tile_of[where] = t
            first_of[where] = jnp.where(j == 0, 1, 0)
            mirror_of[where] = at + steps - 1 - j
            live_of[where] = lens[t] - j * STEP
            return c

        lax.fori_loop(0, steps, list_step, 0)
        return at + steps

    count = lax.fori_loop(0, tiles, list_tile, 0)

    unpack_rows(pairs, rows, peers)
    rows[peers * 64:, :] = jnp.zeros((8, LANE), F32)

    def clear(i, c):
        for acc in accs:
            acc[pl.ds(pl.multiple_of(i * 64, 64), 64), :] = jnp.zeros((64, LANE), F32)
        return c

    lax.fori_loop(0, peers, clear, 0)
    tgt[...] = target[...].astype(F32)
    splats[...] = jnp.zeros_like(splats)
    feat_t[0:2] = jnp.zeros((2, ROW, STEP), BF16)
    geo[0:2] = jnp.zeros((2, 16, STEP), F32)

    prefix = prefix_mat[...]
    suffix = suffix_mat[...]
    sub16 = lax.broadcasted_iota(jnp.int32, (16, STEP), 0).astype(F32) + 0.5
    lane256 = lax.broadcasted_iota(jnp.int32, (1, STEP), 1)
    feature = lax.broadcasted_iota(jnp.int32, (64, PIX), 0) < FEATS

    def scatter(s):
        base = base_of[mirror_of[s + PAD] + PAD]
        base = jnp.where(live_of[s + PAD] > 0, base, tiles * entries)
        for q in range(0, STEP, ACCS):
            ids = [lists[base + q + k] for k in range(ACCS)]
            old = [accs[k][pl.ds(ids[k], 1), :] for k in range(ACCS)]
            for k in range(ACCS):
                accs[k][pl.ds(ids[k], 1), :] = old[k] + grows[q + k:q + k + 1, :]

    def turn_back():
        for k in range(2):
            part = jnp.concatenate(
                [grow_t[:, k * LANE:(k + 1) * LANE], jnp.zeros((64, LANE), F32)], axis=0
            )
            grows[k * LANE:(k + 1) * LANE, :] = jnp.transpose(part)

    def coords(g):
        return sub16 - geo[g, 0:1, :], sub16 - geo[g, 1:2, :]

    def backward(b):
        f = mirror_of[b + PAD]
        g = f + 2
        slot = lax.rem(g, RING)
        t = tile_of[b + PAD]
        keep = first_of[b + PAD] == 0
        dx, dy = coords(g)
        ft = feat_t[g]
        halves = weights[slot]
        d_weight = dot(pull_t[t], jnp.concatenate([ft, ft], axis=0))
        quads = dot(pull_rows[t], halves)
        quads = quads[:64] + quads[64:]
        later = jnp.where(keep, later_ref[...], 0.0)
        sums = [None, None]
        for k in (1, 0):
            cut = slice(k * LANE, (k + 1) * LANE)
            weight = (
                halves[:, 2 * k * LANE:(2 * k + 1) * LANE].astype(F32)
                + halves[:, (2 * k + 1) * LANE:(2 * k + 2) * LANE].astype(F32)
            )
            prod = weight * d_weight[:, cut]
            both = dot(jnp.concatenate(split(prod), axis=1), suffix)
            h = prod - ratio[slot, :, cut] * (both[:, :LANE] + later)
            later = later + both[:, LANE:]
            h = h.reshape(16, 16, LANE)
            dyk = dy[:, cut]
            hy = h * dyk[:, None, :]
            sums[k] = (
                jnp.sum(h, axis=0),
                jnp.sum(hy, axis=0),
                jnp.sum(hy * dyk[:, None, :], axis=0),
            )
        later_ref[...] = later
        s0, s1, s2 = (jnp.concatenate([sums[0][j], sums[1][j]], axis=1) for j in range(3))
        sx = s0 * dx
        m0, mx, my, mxx, mxy, myy = (
            jnp.sum(m, axis=0, keepdims=True) for m in (s0, sx, s1, sx * dx, s1 * dx, s2)
        )
        ca, cb, cc = geo[g, 6:7, :], geo[g, 7:8, :], geo[g, 8:9, :]
        du = (ca * mx + cb * my) * geo[g, 9:10, :]
        dw = (cb * mx + cc * my) * geo[g, 10:11, :]
        shared = -0.5 * cb * mxy
        first = jnp.concatenate(
            [quads[:, 0:LANE] + quads[:, LANE:2 * LANE],
             quads[:, 2 * LANE:3 * LANE] + quads[:, 3 * LANE:]], axis=1
        )
        grow_t[0:56, :] = first[0:56]
        grow_t[56:57, :] = first[56:57]
        outs = (
            du * cam[0, 0] + dw * cam[1, 0],
            du * cam[0, 1] + dw * cam[1, 1],
            du * cam[0, 2] + dw * cam[1, 2],
            -0.5 * ca * mxx + shared,
            -0.5 * cc * myy + shared,
            -mxy * geo[g, 11:12, :],
            geo[g, 12:13, :] * m0,
        )
        for j, value in enumerate(outs):
            grow_t[57 + j:58 + j, :] = value

    def pull(p):
        t = tile_of[p + PAD]
        picture = pic[...]
        for h in range(2):
            image[h, pl.ds(t, FEATS, stride=tiles), :] = picture[:FEATS, h * LANE:(h + 1) * LANE]
        want = jnp.concatenate(
            [tgt[h, pl.ds(t, FEATS, stride=tiles), :] for h in range(2)], axis=1
        )
        want = jnp.concatenate([want, jnp.zeros((64 - FEATS, PIX), F32)], axis=0)
        diff = jnp.where(feature, picture - want, 0.0)
        hi, lo = split(diff)
        both = jnp.concatenate([hi, lo], axis=0)
        pull_rows[t] = both
        pull_t[t] = jnp.transpose(both.astype(F32)).astype(BF16)

    def forward(f):
        g = f + 2
        slot = lax.rem(g, RING)
        keep = first_of[f + PAD] == 0
        dx, dy = coords(g)
        qa = geo[g, 2:3, :] * dx * dx
        qb = geo[g, 3:4, :] * dx
        qc = geo[g, 4:5, :] * dy * dy + geo[g, 5:6, :]
        entering = jnp.where(keep, entering_ref[...], 0.0)
        parts = []
        for k in range(2):
            cut = slice(k * LANE, (k + 1) * LANE)
            power = qa[None, :, cut] + qb[None, :, cut] * dy[:, None, cut] + qc[:, None, cut]
            alpha = jnp.exp2(power.reshape(PIX, LANE))
            logs = jnp.log2(1.0 - alpha)
            both = dot(jnp.concatenate(split(logs), axis=1), prefix)
            weight = alpha * jnp.exp2(both[:, :LANE] + entering)
            entering = entering + both[:, LANE:]
            ratio[slot, :, cut] = alpha * jnp.exp2(-logs)
            parts.extend(split(weight))
        entering_ref[...] = entering
        halves = jnp.concatenate(parts, axis=1)
        weights[slot] = halves
        ft = feat_t[g]
        left, right = ft[:, :LANE], ft[:, LANE:]
        pic[...] = jnp.where(keep, pic[...], 0.0) + dot_t(
            jnp.concatenate([left, left, right, right], axis=1), halves
        )

    def prepare(x):
        g = x + 2
        turned = [
            jnp.transpose(splats[k * LANE:(k + 1) * LANE, :])[0:64] for k in range(2)
        ]
        turned = jnp.concatenate(turned, axis=1)
        feat_t[g] = turned.astype(BF16)
        px, py, pz, sa, sc, sb, so = (turned[57 + j:58 + j, :] for j in range(7))
        tu = jnp.tanh(px * cam[0, 0] + py * cam[0, 1] + pz * cam[0, 2] + cam[0, 3])
        tw = jnp.tanh(px * cam[1, 0] + py * cam[1, 1] + pz * cam[1, 2] + cam[1, 3])
        ca, cc = jnp.exp(sa), jnp.exp(sc)
        tb = jnp.tanh(sb)
        root = 0.9 * jnp.sqrt(ca * cc)
        cb = tb * root
        soft = jnp.exp(-jnp.abs(so))
        log_o = jnp.minimum(so, 0.0) * LOG2E - jnp.log2(1.0 + soft)
        half = -0.5 * LOG2E
        values = (
            8.0 + 6.0 * tu,
            8.0 + 6.0 * tw,
            half * ca,
            (2.0 * half) * cb,
            half * cc,
            jnp.where(lane256 < live_of[x + PAD], log_o, -1e30),
            ca,
            cb,
            cc,
            6.0 * (1.0 - tu * tu),
            6.0 * (1.0 - tw * tw),
            root * (1.0 - tb * tb),
            jnp.where(so >= 0.0, soft, 1.0) / (1.0 + soft),
        )
        for j, value in enumerate(values):
            geo[g, j:j + 1, :] = value

    def gather(n):
        base = base_of[n + PAD]
        for q in range(0, STEP, 32):
            got = [rows[pl.ds(lists[base + q + j], 1), :] for j in range(32)]
            for j in range(32):
                splats[q + j:q + j + 1, :] = got[j]

    def opening(n, c):
        pull(n - 3)
        forward(n - 2)
        prepare(n - 1)
        gather(n)
        return c

    def middle(n, c):
        scatter(n - 9)
        turn_back()
        backward(n - 7)
        pull(n - 3)
        forward(n - 2)
        prepare(n - 1)
        gather(n)
        return c

    def closing(n, c):
        scatter(n - 9)
        turn_back()
        backward(n - 7)
        return c

    lax.fori_loop(0, 7, opening, 0)
    lax.fori_loop(7, count + 3, middle, 0)
    lax.fori_loop(count + 3, count + 9, closing, 0)
    pack_rows(accs, out_pairs, peers)


def triangles():
    r = lax.broadcasted_iota(jnp.int32, (PIX, PIX), 0) % LANE
    c = lax.broadcasted_iota(jnp.int32, (PIX, PIX), 1)
    prefix = (c >= LANE) | (r < c)
    suffix = (c >= LANE) | (r > c)
    return prefix.astype(BF16), suffix.astype(BF16)


def render(lens, lists, cam, pairs, target):
    tiles, entries = lists.shape
    peers = pairs.shape[0] // 32
    steps = tiles * (entries // STEP)
    live = lax.broadcasted_iota(jnp.int32, lists.shape, 1) < lens[:, None]
    flat = jnp.where(live, lists, peers * 64).reshape(-1)
    flat = jnp.concatenate([flat, jnp.full((entries,), peers * 64, jnp.int32)])
    smem = pl.BlockSpec(memory_space=pltpu.SMEM)
    vmem = pl.BlockSpec(memory_space=pltpu.VMEM)
    prefix, suffix = triangles()
    t2 = jnp.transpose(target, (1, 0, 2)).reshape(FEATS * tiles, PIX)
    t2 = jnp.stack([t2[:, :LANE], t2[:, LANE:]])
    image, grads = pl.pallas_call(
        tiles_kernel,
        out_shape=(
            jax.ShapeDtypeStruct((2, FEATS * tiles, LANE), F32),
            jax.ShapeDtypeStruct((peers * 32, LANE), F32),
        ),
        in_specs=[smem] * 3 + [vmem] * 4,
        out_specs=(vmem, vmem),
        scratch_shapes=[
            *[pltpu.SMEM((steps + 2 * PAD,), jnp.int32)] * 5,
            *[pltpu.VMEM((peers * 64 + 8, LANE), F32)] * (1 + ACCS),
            pltpu.VMEM((STEP, LANE), F32),
            pltpu.VMEM((STEP, LANE), F32),
            pltpu.VMEM((steps + 4, ROW, STEP), BF16),
            pltpu.VMEM((steps + 4, 16, STEP), F32),
            pltpu.VMEM((RING, PIX, 2 * STEP), BF16),
            pltpu.VMEM((RING, PIX, STEP), F32),
            pltpu.VMEM((PIX, LANE), F32),
            pltpu.VMEM((PIX, LANE), F32),
            pltpu.VMEM((64, PIX), F32),
            pltpu.VMEM((2, FEATS * tiles, LANE), F32),
            pltpu.VMEM((tiles, 2 * ROW, PIX), BF16),
            pltpu.VMEM((tiles, PIX, 2 * ROW), BF16),
            pltpu.VMEM((ROW, STEP), F32),
        ],
        compiler_params=pltpu.CompilerParams(vmem_limit_bytes=52 << 20),
    )(lens, flat, cam, pairs, t2, prefix, suffix)
    image = jnp.concatenate([image[0], image[1]], axis=1).reshape(FEATS, tiles, PIX)
    return jnp.transpose(image, (1, 0, 2)), grads


def serve_kernel(slot_major, table_lo, served):
    peers = slot_major.shape[1]
    lane = lax.broadcasted_iota(jnp.int32, (64, LANE), 1)
    upper = lane // 64
    mat = table_lo[...]

    def step(g, c):
        ids = pltpu.roll(slot_major[...], lax.rem(peers - g * 8, peers), 1)
        for k in range(8):
            col = jnp.broadcast_to(ids[:, k:k + 1], (64, LANE))
            low = col & 255
            high = (col >> 8) - upper
            hot = [jnp.where(low == lane + q * LANE, 1.0, 0.0).astype(BF16) for q in range(2)]
            got = dot_t(jnp.concatenate(hot, axis=1), mat)
            total = jnp.zeros((64, LANE), F32)
            for q in range(4):
                total = total + jnp.where(high == 2 * q, got[:, q * LANE:(q + 1) * LANE], 0.0)
            total = total + pltpu.roll(total, 64, 1)
            out = jnp.where(lane[:32] < 64, total[:32], total[32:])
            served[pl.ds(pl.multiple_of((g * 8 + k) * 32, 32), 32), :] = out.astype(BF16)
        return c

    lax.fori_loop(0, peers // 8, step, 0)


def serve(incoming, table):
    peers = incoming.shape[0]
    turned = jnp.transpose(table)
    turned = jnp.concatenate([turned[ROW - FEATS:], turned[:ROW - FEATS]], axis=0)
    turned = turned.reshape(ROW, 8, PIX).transpose(1, 0, 2).reshape(8 * ROW, PIX)
    vmem = pl.BlockSpec(memory_space=pltpu.VMEM)
    return pl.pallas_call(
        serve_kernel,
        out_shape=jax.ShapeDtypeStruct((peers * 32, LANE), BF16),
        in_specs=[vmem, vmem],
        out_specs=vmem,
        compiler_params=pltpu.CompilerParams(vmem_limit_bytes=32 << 20),
    )(jnp.transpose(incoming), turned)


def collect_kernel(slot_major, flat, pairs, owned, total):
    peers = slot_major.shape[1]
    lane = lax.broadcasted_iota(jnp.int32, (64, LANE), 1)
    upper = lane // 64
    left = lane[:32] < 64
    low_id = lax.broadcasted_iota(jnp.int32, (512, LANE), 0)
    total[...] = jnp.zeros_like(total)

    def step(g, c):
        ids = pltpu.roll(slot_major[...], lax.rem(peers - g * 8, peers), 1)
        hot = []
        for k in range(4):
            row = flat[pl.ds(g * 4 + k, 1), :] & 511
            hot.append(jnp.where(low_id == row, 1.0, 0.0).astype(BF16))
        blocks = []
        for k in range(8):
            high = (jnp.broadcast_to(ids[:, k:k + 1], (64, LANE)) >> 9) - upper
            two = pairs[pl.ds(pl.multiple_of((g * 8 + k) * 32, 32), 32), :]
            other = pltpu.roll(two, 64, 1)
            both = jnp.concatenate(
                [jnp.where(left, two, other), jnp.where(left, other, two)], axis=0
            )
            hi = both.astype(BF16).astype(F32)
            parts = [
                jnp.where(high == 2 * q, part, 0.0).astype(BF16)
                for part in (hi, both - hi)
                for q in range(2)
            ]
            blocks.append(jnp.concatenate(parts, axis=1))
        total[...] += dot(jnp.concatenate(hot, axis=1), jnp.concatenate(blocks, axis=0))
        return c

    lax.fori_loop(0, peers // 8, step, 0)
    whole = jnp.transpose(total[:, :256] + total[:, 256:])
    for q in range(4):
        part = whole[q * 64:(q + 1) * 64]
        owned[:, q * 512:(q + 1) * 512] = jnp.concatenate([part[FEATS:], part[:FEATS]], axis=0)


def collect(incoming, pairs, rows):
    peers = incoming.shape[0]
    vmem = pl.BlockSpec(memory_space=pltpu.VMEM)
    owned = pl.pallas_call(
        collect_kernel,
        out_shape=jax.ShapeDtypeStruct((ROW, rows), F32),
        in_specs=[vmem] * 3,
        out_specs=vmem,
        scratch_shapes=[pltpu.VMEM((512, 512), F32)],
        compiler_params=pltpu.CompilerParams(vmem_limit_bytes=32 << 20),
    )(jnp.transpose(incoming), incoming.reshape(-1, LANE), pairs)
    return jnp.transpose(owned)


def exchange(x):
    return lax.all_to_all(x, ("gauss", "view"), split_axis=0, concat_axis=0, tiled=True)


def shards(table, view_proj, lengths, lists, requests, target):
    incoming = exchange(requests[0, 0])
    peers = incoming.shape[0]
    served = serve(incoming, table)
    pairs = exchange(served.reshape(peers, 32, LANE)).reshape(peers * 32, LANE)
    image, grads = render(lengths[0], lists[0], view_proj[0], pairs, target[0])
    returned = exchange(grads.reshape(peers, 32, LANE)).reshape(peers * 32, LANE)
    return image[None], collect(incoming, returned, table.shape[0])


def solution(mesh):
    return jax.shard_map(
        shards,
        mesh=mesh,
        in_specs=(
            P(("gauss", "view"), None),
            P("view", None, None),
            P("view", "gauss"),
            P("view", "gauss", None),
            P("view", "gauss", None, None),
            P("view", "gauss", None, None),
        ),
        out_specs=(P("view", "gauss", None, None), P(("gauss", "view"), None)),
        check_vma=False,
    )
```

time: 225 us -> 185 us (0.82); the launches traced: 229 us -> 186 us
  Pallas kernels: 117 us -> 94.3 us
  starting transfers between devices: 49.8 us -> 29 us
    pallas_call x1, Pallas kernels: 90.2 us -> 67.8 us  [render(): pl.pallas_call(tiles_kernel, out_shape=(jax.ShapeDtypeStruct((2, FEATS *...]
    all_to_all x3, starting transfers between devices: 49.8 us -> 29 us  [exchange(): lax.all_to_all(x, ('gauss', 'view'), split_axis=0, concat_axis=0, tiled=T...]
  transfers between devices with their start and end apart: 3 -> 3, of which waited for: 3 -> 3; matrix products, arithmetic and copies ran while one was open for 2% -> 3% of each run, Pallas kernels for 0% -> 0%
where the time goes in v2:
time: 185 us; the launch traced here: 186 us
  Pallas kernels  94.3 us (51%)
  waiting for transfers between devices  53 us (29%)
  starting transfers between devices  29 us (16%)
  local copies, waits for them, and re-layouts  5.88 us (3%)
  other arithmetic  2.82 us (2%)
    pallas_call x1, Pallas kernels, render(): pl.pallas_call(tiles_kernel, out_shape=(jax.ShapeDtypeStruct((2, FEATS *...  67.8 us
    all_to_all x3, waiting for transfers between devices, exchange(): lax.all_to_all(x, ('gauss', 'view'), split_axis=0, concat_axis=0, tiled=T...  53 us
    all_to_all x3, starting transfers between devices, exchange(): lax.all_to_all(x, ('gauss', 'view'), split_axis=0, concat_axis=0, tiled=T...  29 us
    pallas_call x1, Pallas kernels, serve(): pl.pallas_call(serve_kernel, out_shape=jax.ShapeDtypeStruct((peers * 32,...  15.8 us
    pallas_call x1, Pallas kernels, collect(): pl.pallas_call(collect_kernel, out_shape=jax.ShapeDtypeStruct((ROW, rows)...  10.7 us
  transfers between devices with their start and end apart: 3, of which 3 were waited for; matrix products, arithmetic and copies ran while one was open for 3% of the time, Pallas kernels for 0%

profile of v2, /device:TPU:1, one launch (start us, length us, event | category | flops | bytes accessed | tf_op | source)
XLA Modules:
  0.0 185.7 jit_solution(13986572197227804255)
XLA Ops:
  0.6 1.5 copy.12
  2.1 11.5 %all-to-all-start = ((s32[128,1,64]{2,1,0:T(1,128)}), s32[128,1,64]{2,1,0:T(1,128)S(1)}, u32[]{:S(2)}, u32[]{:S(2)}) async-start(s32[128,1,64]{2,1,0:T(1,128)} %bitcast.2), calls=%async_computation | async-start | bytes 131072 | tf_op jit(solution)/shard_map/all_to_all | solution.py:466
  13.6 0.8 slice.25
  14.4 1.0 slice.24
  15.4 0.7 fusion.4
  16.2 0.9 copy.17
  17.1 0.0 copy-start.3
  17.1 6.0 %all-to-all-done = s32[128,1,64]{2,1,0:T(1,128)S(1)} async-done(((s32[128,1,64]{2,1,0:T(1,128)}), s32[128,1,64]{2,1,0:T(1,128)S(1)}, u32[]{:S(2)}, u32[]{:S(2)}) %all-to-all-start) | async-done | bytes 32800 | tf_op jit(solution)/shard_map/all_to_all | solution.py:466
  23.0 0.1 copy.13
  23.1 15.8 %shard_map.77 = bf16[4096,128]{1,0:T(8,128)(2,1)} custom-call(s32[64,128]{1,0:T(8,128)S(1)} %bitcast.41, bf16[512,256]{1,0:T(8,128)(2,1)S(1)} %bitcast.40), custom_call_target="tpu_custom_call" | custom-call | tf_op jit(solution)/shard_map/pallas_call | solution.py:403
  38.9 0.0 copy-start
  38.9 0.0 copy-start.1
  38.9 4.6 %all-to-all-start.1 = ((bf16[128,32,128]{2,1,0:T(8,128)(2,1)}), bf16[128,32,128]{2,1,0:T(8,128)(2,1)S(1)}, u32[]{:S(2)}, u32[]{:S(2)}) async-start(bf16[128,32,128]{2,1,0:T(8,128)(2,1)} %bitcast.8), calls=%async_computation.1 | async-start | bytes 2097152 | tf_op jit(solution)/shard_map/all_to_all | solution.py:466
  43.6 0.0 copy-done.3
  43.7 0.2 fusion.3
  43.9 19.0 %all-to-all-done.1 = bf16[128,32,128]{2,1,0:T(8,128)(2,1)S(1)} async-done(((bf16[128,32,128]{2,1,0:T(8,128)(2,1)}), bf16[128,32,128]{2,1,0:T(8,128)(2,1)S(1)}, u32[]{:S(2)}, u32[]{:S(2)}) %all-to-all-start.1) | async-done | bytes 1048608 | tf_op jit(solution)/shard_map/all_to_all | solution.py:466
  62.9 0.0 copy-start.2
  62.9 1.0 copy-done.2
  63.9 0.0 copy-done
  63.9 0.0 copy-done.1
  63.9 67.8 %shard_map.78 = (f32[2,912,128]{2,1,0:T(8,128)S(1)}, f32[4096,128]{1,0:T(8,128)}) custom-call(s32[16]{0:T(128)S(1)} %bitcast.44, s32[17408]{0:T(1024)S(1)} %concatenate.14.lists, f32[2,4]{1,0:T(2,128)S(1)} %bitcast.45, bf16[4096,128]{1,0:T(8,128)(2,1)} %bitcast.46, bf16[2,912,128]{2,1,0:T(8,128)(2,1)S(1)} %pad_maximum_fusion.target, ...), custom_call_target="tpu_custom_call" | custom-call | tf_op jit(solution)/shard_map/pallas_call | solution.py:341
  131.7 12.9 %all-to-all-start.2 = ((f32[128,32,128]{2,1,0:T(8,128)}), f32[128,32,128]{2,1,0:T(8,128)S(1)}, u32[]{:S(2)}, u32[]{:S(2)}) async-start(f32[128,32,128]{2,1,0:T(8,128)} %bitcast.47), calls=%async_computation.2 | async-start | bytes 4194304 | tf_op jit(solution)/shard_map/all_to_all | solution.py:466
  144.5 0.5 broadcast.31
  145.1 0.8 reduce.3
  145.9 0.1 reshape.48.flat
  145.9 0.1 fusion.6
  146.0 1.0 maximum_bitcast_fusion
  147.0 28.0 %all-to-all-done.2 = f32[128,32,128]{2,1,0:T(8,128)S(1)} async-done(((f32[128,32,128]{2,1,0:T(8,128)}), f32[128,32,128]{2,1,0:T(8,128)S(1)}, u32[]{:S(2)}, u32[]{:S(2)}) %all-to-all-start.2) | async-done | bytes 2097184 | tf_op jit(solution)/shard_map/all_to_all | solution.py:466
  175.1 10.7 %shard_map.79 = f32[64,2048]{1,0:T(8,128)} custom-call(s32[64,128]{1,0:T(8,128)S(1)} %bitcast.42, s32[64,128]{1,0:T(8,128)S(1)} %reshape.48.flat, f32[4096,128]{1,0:T(8,128)S(1)} %bitcast.39), custom_call_target="tpu_custom_call" | custom-call | tf_op jit(solution)/shard_map/pallas_call | solution.py:454
  (9 shorter events, 0.2 us)
Async XLA Ops:
  2.1 20.9 %all-to-all-start = ((s32[128,1,64]{2,1,0:T(1,128)}), s32[128,1,64]{2,1,0:T(1,128)S(1)}, u32[]{:S(2)}, u32[]{:S(2)}) async-start(s32[128,1,64]{2,1,0:T(1,128)} %bitcast.2), calls=%async_computation | async-start | bytes 131072 | tf_op jit(solution)/shard_map/all_to_all | solution.py:466
  17.1 26.6 %copy-start.3 = (bf16[1,16,57,256]{3,1,2,0:T(8,128)(2,1)S(1)}, bf16[1,16,57,256]{3,1,2,0:T(8,128)(2,1)}, u32[]{:S(2)}) copy-start(bf16[1,16,57,256]{3,1,2,0:T(8,128)(2,1)} %param.11) | copy-start | bytes 1400836
  38.9 24.9 %copy-start = (s32[1,16]{1,0:T(1,128)S(1)}, s32[1,16]{1,0:T(1,128)}, u32[]{:S(2)}) copy-start(s32[1,16]{1,0:T(1,128)} %param.8) | copy-start | bytes 196
  38.9 24.9 %copy-start.1 = (f32[1,2,4]{2,1,0:T(2,128)S(1)}, f32[1,2,4]{2,1,0:T(2,128)}, u32[]{:S(2)}) copy-start(f32[1,2,4]{2,1,0:T(2,128)} %param.7) | copy-start | bytes 100
  38.9 24.0 %all-to-all-start.1 = ((bf16[128,32,128]{2,1,0:T(8,128)(2,1)}), bf16[128,32,128]{2,1,0:T(8,128)(2,1)S(1)}, u32[]{:S(2)}, u32[]{:S(2)}) async-start(bf16[128,32,128]{2,1,0:T(8,128)(2,1)} %bitcast.8), calls=%async_computation.1 | async-start | bytes 2097152 | tf_op jit(solution)/shard_map/all_to_all | solution.py:466
  62.9 1.0 copy-start.2
  131.7 43.4 %all-to-all-start.2 = ((f32[128,32,128]{2,1,0:T(8,128)}), f32[128,32,128]{2,1,0:T(8,128)S(1)}, u32[]{:S(2)}, u32[]{:S(2)}) async-start(f32[128,32,128]{2,1,0:T(8,128)} %bitcast.47), calls=%async_computation.2 | async-start | bytes 4194304 | tf_op jit(solution)/shard_map/all_to_all | solution.py:466

commit v3 on v2

--- a/solution.py
+++ b/solution.py
@@ -1,3 +1,5 @@
+import functools
+
 import functools
 
 import jax
@@ -16,6 +18,7 @@
 STEP = 256
 RING = 9
 PAD = 16
+DRIP = 6
 F32 = jnp.float32
 BF16 = jnp.bfloat16
 
@@ -71,6 +74,8 @@
     base_of, tile_of, first_of, mirror_of, live_of,
     rows, acc0, acc1, acc2, acc3,
     splats, grows, feat_t, geo, weights, ratio, entering_ref, later_ref, pic, tgt, pull_rows, pull_t, grow_t,
+    feat_new, geo_new, weights_new, ratio_new, rows_new, cols_new,
+    dy_back, dy_front, qc_front, wide, wide_new,
 ):
     accs = (acc0, acc1, acc2, acc3)
     tiles = lens.shape[0]
@@ -115,8 +120,8 @@
     lax.fori_loop(0, peers, clear, 0)
     tgt[...] = target[...].astype(F32)
     splats[...] = jnp.zeros_like(splats)
-    feat_t[0:2] = jnp.zeros((2, ROW, STEP), BF16)
-    geo[0:2] = jnp.zeros((2, 16, STEP), F32)
+    feat_new[...] = jnp.zeros_like(feat_new)
+    geo_new[...] = jnp.zeros_like(geo_new)
 
     prefix = prefix_mat[...]
     suffix = suffix_mat[...]
@@ -127,11 +132,14 @@
     def scatter(s):
         base = base_of[mirror_of[s + PAD] + PAD]
         base = jnp.where(live_of[s + PAD] > 0, base, tiles * entries)
-        for q in range(0, STEP, ACCS):
+
+        def rows_from(q):
             ids = [lists[base + q + k] for k in range(ACCS)]
             old = [accs[k][pl.ds(ids[k], 1), :] for k in range(ACCS)]
             for k in range(ACCS):
                 accs[k][pl.ds(ids[k], 1), :] = old[k] + grows[q + k:q + k + 1, :]
+
+        return [functools.partial(rows_from, q) for q in range(0, STEP, ACCS)]
 
     def turn_back():
         for k in range(2):
@@ -143,13 +151,17 @@
     def coords(g):
         return sub16 - geo[g, 0:1, :], sub16 - geo[g, 1:2, :]
 
-    def backward(b):
+    def spread(ref, cut):
+        return jnp.stack([jnp.broadcast_to(ref[y:y + 1, cut], (16, LANE)) for y in range(16)])
+
+    def backward(b, drip):
         f = mirror_of[b + PAD]
         g = f + 2
         slot = lax.rem(g, RING)
         t = tile_of[b + PAD]
         keep = first_of[b + PAD] == 0
         dx, dy = coords(g)
+        dy_back[...] = dy
         ft = feat_t[g]
         halves = weights[slot]
         d_weight = dot(pull_t[t], jnp.concatenate([ft, ft], axis=0))
@@ -159,21 +171,22 @@
         sums = [None, None]
         for k in (1, 0):
             cut = slice(k * LANE, (k + 1) * LANE)
-            weight = (
-                halves[:, 2 * k * LANE:(2 * k + 1) * LANE].astype(F32)
-                + halves[:, (2 * k + 1) * LANE:(2 * k + 2) * LANE].astype(F32)
-            )
-            prod = weight * d_weight[:, cut]
+            prod = wide[slot, :, cut] * d_weight[:, cut]
+            drip()
             both = dot(jnp.concatenate(split(prod), axis=1), suffix)
+            drip()
             h = prod - ratio[slot, :, cut] * (both[:, :LANE] + later)
+            drip()
             later = later + both[:, LANE:]
+            drip()
             h = h.reshape(16, 16, LANE)
-            dyk = dy[:, cut]
-            hy = h * dyk[:, None, :]
+            dyk = spread(dy_back, cut)
+            hy = h * dyk
+            drip()
             sums[k] = (
                 jnp.sum(h, axis=0),
                 jnp.sum(hy, axis=0),
-                jnp.sum(hy * dyk[:, None, :], axis=0),
+                jnp.sum(hy * dyk, axis=0),
             )
         later_ref[...] = later
         s0, s1, s2 = (jnp.concatenate([sums[0][j], sums[1][j]], axis=1) for j in range(3))
@@ -215,32 +228,40 @@
         diff = jnp.where(feature, picture - want, 0.0)
         hi, lo = split(diff)
         both = jnp.concatenate([hi, lo], axis=0)
-        pull_rows[t] = both
-        pull_t[t] = jnp.transpose(both.astype(F32)).astype(BF16)
-
-    def forward(f):
+        rows_new[...] = both
+        cols_new[...] = jnp.transpose(both.astype(F32)).astype(BF16)
+
+    def forward(f, drip):
         g = f + 2
-        slot = lax.rem(g, RING)
         keep = first_of[f + PAD] == 0
         dx, dy = coords(g)
         qa = geo[g, 2:3, :] * dx * dx
         qb = geo[g, 3:4, :] * dx
         qc = geo[g, 4:5, :] * dy * dy + geo[g, 5:6, :]
+        dy_front[...] = dy
+        qc_front[...] = qc
         entering = jnp.where(keep, entering_ref[...], 0.0)
         parts = []
         for k in range(2):
             cut = slice(k * LANE, (k + 1) * LANE)
-            power = qa[None, :, cut] + qb[None, :, cut] * dy[:, None, cut] + qc[:, None, cut]
+            power = qa[None, :, cut] + qb[None, :, cut] * spread(dy_front, cut) + spread(qc_front, cut)
             alpha = jnp.exp2(power.reshape(PIX, LANE))
-            logs = jnp.log2(1.0 - alpha)
+            drip()
+            rest = 1.0 - alpha
+            logs = jnp.log2(rest)
+            drip()
             both = dot(jnp.concatenate(split(logs), axis=1), prefix)
+            drip()
             weight = alpha * jnp.exp2(both[:, :LANE] + entering)
+            drip()
             entering = entering + both[:, LANE:]
-            ratio[slot, :, cut] = alpha * jnp.exp2(-logs)
+            ratio_new[:, cut] = alpha * pl.reciprocal(rest, approx=True)
+            wide_new[:, cut] = weight
             parts.extend(split(weight))
+            drip()
         entering_ref[...] = entering
         halves = jnp.concatenate(parts, axis=1)
-        weights[slot] = halves
+        weights_new[...] = halves
         ft = feat_t[g]
         left, right = ft[:, :LANE], ft[:, LANE:]
         pic[...] = jnp.where(keep, pic[...], 0.0) + dot_t(
@@ -248,12 +269,11 @@
         )
 
     def prepare(x):
-        g = x + 2
         turned = [
             jnp.transpose(splats[k * LANE:(k + 1) * LANE, :])[0:64] for k in range(2)
         ]
         turned = jnp.concatenate(turned, axis=1)
-        feat_t[g] = turned.astype(BF16)
+        feat_new[...] = turned.astype(BF16)
         px, py, pz, sa, sc, sb, so = (turned[57 + j:58 + j, :] for j in range(7))
         tu = jnp.tanh(px * cam[0, 0] + py * cam[0, 1] + pz * cam[0, 2] + cam[0, 3])
         tw = jnp.tanh(px * cam[1, 0] + py * cam[1, 1] + pz * cam[1, 2] + cam[1, 3])
@@ -280,41 +300,71 @@
             jnp.where(so >= 0.0, soft, 1.0) / (1.0 + soft),
         )
         for j, value in enumerate(values):
-            geo[g, j:j + 1, :] = value
+            geo_new[j:j + 1, :] = value
 
     def gather(n):
         base = base_of[n + PAD]
-        for q in range(0, STEP, 32):
-            got = [rows[pl.ds(lists[base + q + j], 1), :] for j in range(32)]
-            for j in range(32):
+
+        def rows_from(q):
+            got = [rows[pl.ds(lists[base + q + j], 1), :] for j in range(4)]
+            for j in range(4):
                 splats[q + j:q + j + 1, :] = got[j]
 
+        return [functools.partial(rows_from, q) for q in range(0, STEP, 4)]
+
+    def file(n):
+        feat_t[n] = feat_new[...]
+        geo[n] = geo_new[...]
+        slot = lax.rem(n + RING - 1, RING)
+        weights[slot] = weights_new[...]
+        ratio[slot] = ratio_new[...]
+        wide[slot] = wide_new[...]
+        t = tile_of[n - 4 + PAD]
+        pull_rows[t] = rows_new[...]
+        pull_t[t] = cols_new[...]
+
+    moves = []
+
+    def drip(share=1.0):
+        for _ in range(min(len(moves), max(1, int(DRIP * share)))):
+            moves.pop(0)()
+
+    def flush():
+        while moves:
+            moves.pop(0)()
+
     def opening(n, c):
+        file(n)
         pull(n - 3)
-        forward(n - 2)
         prepare(n - 1)
-        gather(n)
+        moves.extend(gather(n))
+        forward(n - 2, drip)
+        flush()
         return c
 
     def middle(n, c):
-        scatter(n - 9)
+        file(n)
         turn_back()
-        backward(n - 7)
         pull(n - 3)
-        forward(n - 2)
         prepare(n - 1)
-        gather(n)
+        for pair in zip(scatter(n - 8), gather(n)):
+            moves.extend(pair)
+        backward(n - 7, drip)
+        forward(n - 2, drip)
+        flush()
         return c
 
     def closing(n, c):
-        scatter(n - 9)
         turn_back()
-        backward(n - 7)
+        moves.extend(scatter(n - 8))
+        backward(n - 7, drip)
+        flush()
         return c
 
     lax.fori_loop(0, 7, opening, 0)
     lax.fori_loop(7, count + 3, middle, 0)
-    lax.fori_loop(count + 3, count + 9, closing, 0)
+    file(count + 3)
+    lax.fori_loop(count + 3, count + 8, closing, 0)
     pack_rows(accs, out_pairs, peers)
 
 
@@ -362,6 +412,15 @@
             pltpu.VMEM((tiles, 2 * ROW, PIX), BF16),
             pltpu.VMEM((tiles, PIX, 2 * ROW), BF16),
             pltpu.VMEM((ROW, STEP), F32),
+            pltpu.VMEM((ROW, STEP), BF16),
+            pltpu.VMEM((16, STEP), F32),
+            pltpu.VMEM((PIX, 2 * STEP), BF16),
+            pltpu.VMEM((PIX, STEP), F32),
+            pltpu.VMEM((2 * ROW, PIX), BF16),
+            pltpu.VMEM((PIX, 2 * ROW), BF16),
+            *[pltpu.VMEM((16, STEP), F32)] * 3,
+            pltpu.VMEM((RING, PIX, STEP), F32),
+            pltpu.VMEM((PIX, STEP), F32),
         ],
         compiler_params=pltpu.CompilerParams(vmem_limit_bytes=52 << 20),
     )(lens, flat, cam, pairs, t2, prefix, suffix)
@@ -373,19 +432,25 @@
     peers = slot_major.shape[1]
     lane = lax.broadcasted_iota(jnp.int32, (64, LANE), 1)
     upper = lane // 64
-    mat = table_lo[...]
+    mat = jnp.transpose(table_lo[...].astype(F32)).astype(BF16)
 
     def step(g, c):
         ids = pltpu.roll(slot_major[...], lax.rem(peers - g * 8, peers), 1)
+        cols = [jnp.broadcast_to(ids[:, k:k + 1], (64, LANE)) for k in range(8)]
+        hot = [
+            jnp.concatenate(
+                [jnp.where((col & 255) == lane + q * LANE, 1.0, 0.0).astype(BF16) for q in range(2)],
+                axis=1,
+            )
+            for col in cols
+        ]
+        got = dot(jnp.concatenate(hot, axis=0), mat)
         for k in range(8):
-            col = jnp.broadcast_to(ids[:, k:k + 1], (64, LANE))
-            low = col & 255
-            high = (col >> 8) - upper
-            hot = [jnp.where(low == lane + q * LANE, 1.0, 0.0).astype(BF16) for q in range(2)]
-            got = dot_t(jnp.concatenate(hot, axis=1), mat)
+            high = (cols[k] >> 8) - upper
             total = jnp.zeros((64, LANE), F32)
             for q in range(4):
-                total = total + jnp.where(high == 2 * q, got[:, q * LANE:(q + 1) * LANE], 0.0)
+                part = got[k * 64:(k + 1) * 64, q * LANE:(q + 1) * LANE]
+                total = total + jnp.where(high == 2 * q, part, 0.0)
             total = total + pltpu.roll(total, 64, 1)
             out = jnp.where(lane[:32] < 64, total[:32], total[32:])
             served[pl.ds(pl.multiple_of((g * 8 + k) * 32, 32), 32), :] = out.astype(BF16)

time: 185 us -> 167 us (0.903); the launches traced: 186 us -> 166 us
  Pallas kernels: 94.3 us -> 81.8 us
  starting transfers between devices: 29 us -> 21.5 us
    all_to_all x3, starting transfers between devices: 29 us -> 21.5 us  [exchange(): lax.all_to_all(x, ('gauss', 'view'), split_axis=0, concat_axis=0, tiled=T...]
    pallas_call x1, Pallas kernels: 15.8 us -> 8.91 us  [serve(): pl.pallas_call(serve_kernel, out_shape=jax.ShapeDtypeStruct((peers * 32,...]
    pallas_call x1, Pallas kernels: 67.8 us -> 62.3 us  [render(): pl.pallas_call(tiles_kernel, out_shape=(jax.ShapeDtypeStruct((2, FEATS *...]
  transfers between devices with their start and end apart: 3 -> 3, of which waited for: 3 -> 3; matrix products, arithmetic and copies ran while one was open for 3% -> 4% of each run, Pallas kernels for 0% -> 0%
where the time goes in v3:
time: 167 us; the launch traced here: 166 us
  Pallas kernels  81.8 us (49%)
  waiting for transfers between devices  53 us (32%)
  starting transfers between devices  21.5 us (13%)
  local copies, waits for them, and re-layouts  5.88 us (4%)
  other arithmetic  2.82 us (2%)
    pallas_call x1, Pallas kernels, render(): pl.pallas_call(tiles_kernel, out_shape=(jax.ShapeDtypeStruct((2, FEATS *...  62.3 us
    all_to_all x3, waiting for transfers between devices, exchange(): lax.all_to_all(x, ('gauss', 'view'), split_axis=0, concat_axis=0, tiled=T...  53 us
    all_to_all x3, starting transfers between devices, exchange(): lax.all_to_all(x, ('gauss', 'view'), split_axis=0, concat_axis=0, tiled=T...  21.5 us
    pallas_call x1, Pallas kernels, collect(): pl.pallas_call(collect_kernel, out_shape=jax.ShapeDtypeStruct((ROW, rows)...  10.7 us
    pallas_call x1, Pallas kernels, serve(): pl.pallas_call(serve_kernel, out_shape=jax.ShapeDtypeStruct((peers * 32,...  8.91 us
  transfers between devices with their start and end apart: 3, of which 3 were waited for; matrix products, arithmetic and copies ran while one was open for 4% of the time, Pallas kernels for 0%

profile of v3, /device:TPU:1, one launch (start us, length us, event | category | flops | bytes accessed | tf_op | source)
XLA Modules:
  0.0 165.8 jit_solution(6004202370375467097)
XLA Ops:
  0.6 1.5 copy.12
  2.1 11.5 %all-to-all-start = ((s32[128,1,64]{2,1,0:T(1,128)}), s32[128,1,64]{2,1,0:T(1,128)S(1)}, u32[]{:S(2)}, u32[]{:S(2)}) async-start(s32[128,1,64]{2,1,0:T(1,128)} %bitcast.2), calls=%async_computation | async-start | bytes 131072 | tf_op jit(solution)/shard_map/all_to_all | solution.py:531
  13.6 0.8 slice.25
  14.4 1.0 slice.24
  15.4 0.7 fusion.4
  16.2 0.9 copy.17
  17.1 0.0 copy-start.3
  17.1 6.0 %all-to-all-done = s32[128,1,64]{2,1,0:T(1,128)S(1)} async-done(((s32[128,1,64]{2,1,0:T(1,128)}), s32[128,1,64]{2,1,0:T(1,128)S(1)}, u32[]{:S(2)}, u32[]{:S(2)}) %all-to-all-start) | async-done | bytes 32800 | tf_op jit(solution)/shard_map/all_to_all | solution.py:531
  23.0 0.1 copy.13
  23.1 8.9 %shard_map.77 = bf16[4096,128]{1,0:T(8,128)(2,1)} custom-call(s32[64,128]{1,0:T(8,128)S(1)} %bitcast.41, bf16[512,256]{1,0:T(8,128)(2,1)S(1)} %bitcast.40), custom_call_target="tpu_custom_call" | custom-call | tf_op jit(solution)/shard_map/pallas_call | solution.py:468
  32.0 0.0 copy-start
  32.0 0.0 copy-start.1
  32.0 4.6 %all-to-all-start.1 = ((bf16[128,32,128]{2,1,0:T(8,128)(2,1)}), bf16[128,32,128]{2,1,0:T(8,128)(2,1)S(1)}, u32[]{:S(2)}, u32[]{:S(2)}) async-start(bf16[128,32,128]{2,1,0:T(8,128)(2,1)} %bitcast.8), calls=%async_computation.1 | async-start | bytes 2097152 | tf_op jit(solution)/shard_map/all_to_all | solution.py:531
  36.7 0.0 copy-done.3
  36.8 0.2 fusion.3
  37.0 19.0 %all-to-all-done.1 = bf16[128,32,128]{2,1,0:T(8,128)(2,1)S(1)} async-done(((bf16[128,32,128]{2,1,0:T(8,128)(2,1)}), bf16[128,32,128]{2,1,0:T(8,128)(2,1)S(1)}, u32[]{:S(2)}, u32[]{:S(2)}) %all-to-all-start.1) | async-done | bytes 1048608 | tf_op jit(solution)/shard_map/all_to_all | solution.py:531
  56.0 0.0 copy-start.2
  56.0 1.0 copy-done.2
  57.0 0.0 copy-done
  57.0 0.0 copy-done.1
  57.0 62.3 %shard_map.78 = (f32[2,912,128]{2,1,0:T(8,128)S(1)}, f32[4096,128]{1,0:T(8,128)}) custom-call(s32[16]{0:T(128)S(1)} %bitcast.44, s32[17408]{0:T(1024)S(1)} %concatenate.14.lists, f32[2,4]{1,0:T(2,128)S(1)} %bitcast.45, bf16[4096,128]{1,0:T(8,128)(2,1)} %bitcast.46, bf16[2,912,128]{2,1,0:T(8,128)(2,1)S(1)} %pad_maximum_fusion.target, ...), custom_call_target="tpu_custom_call" | custom-call | tf_op jit(solution)/shard_map/pallas_call | solution.py:391
  119.2 5.4 %all-to-all-start.2 = ((f32[128,32,128]{2,1,0:T(8,128)}), f32[128,32,128]{2,1,0:T(8,128)S(1)}, u32[]{:S(2)}, u32[]{:S(2)}) async-start(f32[128,32,128]{2,1,0:T(8,128)} %bitcast.47), calls=%async_computation.2 | async-start | bytes 4194304 | tf_op jit(solution)/shard_map/all_to_all | solution.py:531
  124.6 0.5 broadcast.31
  125.2 0.8 reduce.3
  126.0 0.1 reshape.48.flat
  126.0 0.1 fusion.6
  126.1 1.0 maximum_bitcast_fusion
  127.1 28.0 %all-to-all-done.2 = f32[128,32,128]{2,1,0:T(8,128)S(1)} async-done(((f32[128,32,128]{2,1,0:T(8,128)}), f32[128,32,128]{2,1,0:T(8,128)S(1)}, u32[]{:S(2)}, u32[]{:S(2)}) %all-to-all-start.2) | async-done | bytes 2097184 | tf_op jit(solution)/shard_map/all_to_all | solution.py:531
  155.2 10.7 %shard_map.79 = f32[64,2048]{1,0:T(8,128)} custom-call(s32[64,128]{1,0:T(8,128)S(1)} %bitcast.42, s32[64,128]{1,0:T(8,128)S(1)} %reshape.48.flat, f32[4096,128]{1,0:T(8,128)S(1)} %bitcast.39), custom_call_target="tpu_custom_call" | custom-call | tf_op jit(solution)/shard_map/pallas_call | solution.py:519
  (9 shorter events, 0.2 us)
Async XLA Ops:
  2.1 20.9 %all-to-all-start = ((s32[128,1,64]{2,1,0:T(1,128)}), s32[128,1,64]{2,1,0:T(1,128)S(1)}, u32[]{:S(2)}, u32[]{:S(2)}) async-start(s32[128,1,64]{2,1,0:T(1,128)} %bitcast.2), calls=%async_computation | async-start | bytes 131072 | tf_op jit(solution)/shard_map/all_to_all | solution.py:531
  17.1 19.6 %copy-start.3 = (bf16[1,16,57,256]{3,1,2,0:T(8,128)(2,1)S(1)}, bf16[1,16,57,256]{3,1,2,0:T(8,128)(2,1)}, u32[]{:S(2)}) copy-start(bf16[1,16,57,256]{3,1,2,0:T(8,128)(2,1)} %param.11) | copy-start | bytes 1400836
  32.0 24.9 %copy-start = (s32[1,16]{1,0:T(1,128)S(1)}, s32[1,16]{1,0:T(1,128)}, u32[]{:S(2)}) copy-start(s32[1,16]{1,0:T(1,128)} %param.8) | copy-start | bytes 196
  32.0 24.9 %copy-start.1 = (f32[1,2,4]{2,1,0:T(2,128)S(1)}, f32[1,2,4]{2,1,0:T(2,128)}, u32[]{:S(2)}) copy-start(f32[1,2,4]{2,1,0:T(2,128)} %param.7) | copy-start | bytes 100
  32.0 24.0 %all-to-all-start.1 = ((bf16[128,32,128]{2,1,0:T(8,128)(2,1)}), bf16[128,32,128]{2,1,0:T(8,128)(2,1)S(1)}, u32[]{:S(2)}, u32[]{:S(2)}) async-start(bf16[128,32,128]{2,1,0:T(8,128)(2,1)} %bitcast.8), calls=%async_computation.1 | async-start | bytes 2097152 | tf_op jit(solution)/shard_map/all_to_all | solution.py:531
  56.0 1.0 copy-start.2
  119.2 35.9 %all-to-all-start.2 = ((f32[128,32,128]{2,1,0:T(8,128)}), f32[128,32,128]{2,1,0:T(8,128)S(1)}, u32[]{:S(2)}, u32[]{:S(2)}) async-start(f32[128,32,128]{2,1,0:T(8,128)} %bitcast.47), calls=%async_computation.2 | async-start | bytes 4194304 | tf_op jit(solution)/shard_map/all_to_all | solution.py:531

commit v4 on v3

--- a/solution.py
+++ b/solution.py
@@ -75,7 +75,7 @@
     rows, acc0, acc1, acc2, acc3,
     splats, grows, feat_t, geo, weights, ratio, entering_ref, later_ref, pic, tgt, pull_rows, pull_t, grow_t,
     feat_new, geo_new, weights_new, ratio_new, rows_new, cols_new,
-    dy_back, dy_front, qc_front, wide, wide_new,
+    dy_back, dy_front, qc_front, splats_new,
 ):
     accs = (acc0, acc1, acc2, acc3)
     tiles = lens.shape[0]
@@ -119,7 +119,7 @@
 
     lax.fori_loop(0, peers, clear, 0)
     tgt[...] = target[...].astype(F32)
-    splats[...] = jnp.zeros_like(splats)
+    splats_new[...] = jnp.zeros_like(splats_new)
     feat_new[...] = jnp.zeros_like(feat_new)
     geo_new[...] = jnp.zeros_like(geo_new)
 
@@ -171,7 +171,11 @@
         sums = [None, None]
         for k in (1, 0):
             cut = slice(k * LANE, (k + 1) * LANE)
-            prod = wide[slot, :, cut] * d_weight[:, cut]
+            weight = (
+                halves[:, 2 * k * LANE:(2 * k + 1) * LANE].astype(F32)
+                + halves[:, (2 * k + 1) * LANE:(2 * k + 2) * LANE].astype(F32)
+            )
+            prod = weight * d_weight[:, cut]
             drip()
             both = dot(jnp.concatenate(split(prod), axis=1), suffix)
             drip()
@@ -256,7 +260,6 @@
             drip()
             entering = entering + both[:, LANE:]
             ratio_new[:, cut] = alpha * pl.reciprocal(rest, approx=True)
-            wide_new[:, cut] = weight
             parts.extend(split(weight))
             drip()
         entering_ref[...] = entering
@@ -308,7 +311,7 @@
         def rows_from(q):
             got = [rows[pl.ds(lists[base + q + j], 1), :] for j in range(4)]
             for j in range(4):
-                splats[q + j:q + j + 1, :] = got[j]
+                splats_new[q + j:q + j + 1, :] = got[j]
 
         return [functools.partial(rows_from, q) for q in range(0, STEP, 4)]
 
@@ -318,7 +321,6 @@
         slot = lax.rem(n + RING - 1, RING)
         weights[slot] = weights_new[...]
         ratio[slot] = ratio_new[...]
-        wide[slot] = wide_new[...]
         t = tile_of[n - 4 + PAD]
         pull_rows[t] = rows_new[...]
         pull_t[t] = cols_new[...]
@@ -334,6 +336,7 @@
             moves.pop(0)()
 
     def opening(n, c):
+        splats[...] = splats_new[...]
         file(n)
         pull(n - 3)
         prepare(n - 1)
@@ -343,14 +346,19 @@
         return c
 
     def middle(n, c):
+        @pl.when(n > 0)
+        def _():
+            splats[...] = splats_new[...]
+
         file(n)
         turn_back()
+
+        prepare(n - 1)
         pull(n - 3)
-        prepare(n - 1)
         for pair in zip(scatter(n - 8), gather(n)):
             moves.extend(pair)
+        forward(n - 2, drip)
         backward(n - 7, drip)
-        forward(n - 2, drip)
         flush()
         return c
 
@@ -419,8 +427,7 @@
             pltpu.VMEM((2 * ROW, PIX), BF16),
             pltpu.VMEM((PIX, 2 * ROW), BF16),
             *[pltpu.VMEM((16, STEP), F32)] * 3,
-            pltpu.VMEM((RING, PIX, STEP), F32),
-            pltpu.VMEM((PIX, STEP), F32),
+            pltpu.VMEM((STEP, LANE), F32),
         ],
         compiler_params=pltpu.CompilerParams(vmem_limit_bytes=52 << 20),
     )(lens, flat, cam, pairs, t2, prefix, suffix)
@@ -435,8 +442,8 @@
     mat = jnp.transpose(table_lo[...].astype(F32)).astype(BF16)
 
     def step(g, c):
-        ids = pltpu.roll(slot_major[...], lax.rem(peers - g * 8, peers), 1)
-        cols = [jnp.broadcast_to(ids[:, k:k + 1], (64, LANE)) for k in range(8)]
+        ids = pltpu.roll(slot_major[...], lax.rem(peers - g * 32, peers), 1)
+        cols = [jnp.broadcast_to(ids[:, k:k + 1], (64, LANE)) for k in range(32)]
         hot = [
             jnp.concatenate(
                 [jnp.where((col & 255) == lane + q * LANE, 1.0, 0.0).astype(BF16) for q in range(2)],
@@ -445,7 +452,7 @@
             for col in cols
         ]
         got = dot(jnp.concatenate(hot, axis=0), mat)
-        for k in range(8):
+        for k in range(32):
             high = (cols[k] >> 8) - upper
             total = jnp.zeros((64, LANE), F32)
             for q in range(4):
@@ -453,10 +460,10 @@
                 total = total + jnp.where(high == 2 * q, part, 0.0)
             total = total + pltpu.roll(total, 64, 1)
             out = jnp.where(lane[:32] < 64, total[:32], total[32:])
-            served[pl.ds(pl.multiple_of((g * 8 + k) * 32, 32), 32), :] = out.astype(BF16)
-        return c
-
-    lax.fori_loop(0, peers // 8, step, 0)
+            served[pl.ds(pl.multiple_of((g * 32 + k) * 32, 32), 32), :] = out.astype(BF16)
+        return c
+
+    lax.fori_loop(0, peers // 32, step, 0)
 
 
 def serve(incoming, table):
@@ -483,15 +490,15 @@
     total[...] = jnp.zeros_like(total)
 
     def step(g, c):
-        ids = pltpu.roll(slot_major[...], lax.rem(peers - g * 8, peers), 1)
+        ids = pltpu.roll(slot_major[...], lax.rem(peers - g * 32, peers), 1)
         hot = []
-        for k in range(4):
-            row = flat[pl.ds(g * 4 + k, 1), :] & 511
+        for k in range(16):
+            row = flat[pl.ds(g * 16 + k, 1), :] & 511
             hot.append(jnp.where(low_id == row, 1.0, 0.0).astype(BF16))
         blocks = []
-        for k in range(8):
+        for k in range(32):
             high = (jnp.broadcast_to(ids[:, k:k + 1], (64, LANE)) >> 9) - upper
-            two = pairs[pl.ds(pl.multiple_of((g * 8 + k) * 32, 32), 32), :]
+            two = pairs[pl.ds(pl.multiple_of((g * 32 + k) * 32, 32), 32), :]
             other = pltpu.roll(two, 64, 1)
             both = jnp.concatenate(
                 [jnp.where(left, two, other), jnp.where(left, other, two)], axis=0
@@ -506,7 +513,7 @@
         total[...] += dot(jnp.concatenate(hot, axis=1), jnp.concatenate(blocks, axis=0))
         return c
 
-    lax.fori_loop(0, peers // 8, step, 0)
+    lax.fori_loop(0, peers // 32, step, 0)
     whole = jnp.transpose(total[:, :256] + total[:, 256:])
     for q in range(4):
         part = whole[q * 64:(q + 1) * 64]

time: 167 us -> 159 us (0.952)
  Pallas kernels: 81.8 us -> 54.3 us
  starting transfers between devices: 21.5 us -> 41.3 us
    pallas_call x1, Pallas kernels: 62.3 us -> 42.3 us  [render(): pl.pallas_call(tiles_kernel, out_shape=(jax.ShapeDtypeStruct((2, FEATS *...]
    all_to_all x3, starting transfers between devices: 21.5 us -> 41.3 us  [exchange(): lax.all_to_all(x, ('gauss', 'view'), split_axis=0, concat_axis=0, tiled=T...]
    pallas_call x1, Pallas kernels: 8.91 us -> 5.06 us  [serve(): pl.pallas_call(serve_kernel, out_shape=jax.ShapeDtypeStruct((peers * 32,...]
    pallas_call x1, Pallas kernels: 10.7 us -> 6.95 us  [collect(): pl.pallas_call(collect_kernel, out_shape=jax.ShapeDtypeStruct((ROW, rows)...]
where the time goes in v4:
time: 159 us; the launch traced here: 158 us
  Pallas kernels  54.3 us (34%)
  waiting for transfers between devices  53 us (33%)
  starting transfers between devices  41.3 us (26%)
  local copies, waits for them, and re-layouts  5.88 us (4%)
  other arithmetic  2.82 us (2%)
    all_to_all x3, waiting for transfers between devices, exchange(): lax.all_to_all(x, ('gauss', 'view'), split_axis=0, concat_axis=0, tiled=T...  53 us
    pallas_call x1, Pallas kernels, render(): pl.pallas_call(tiles_kernel, out_shape=(jax.ShapeDtypeStruct((2, FEATS *...  42.3 us
    all_to_all x3, starting transfers between devices, exchange(): lax.all_to_all(x, ('gauss', 'view'), split_axis=0, concat_axis=0, tiled=T...  41.3 us
    pallas_call x1, Pallas kernels, collect(): pl.pallas_call(collect_kernel, out_shape=jax.ShapeDtypeStruct((ROW, rows)...  6.95 us
    pallas_call x1, Pallas kernels, serve(): pl.pallas_call(serve_kernel, out_shape=jax.ShapeDtypeStruct((peers * 32,...  5.06 us
    unnamed x11, local copies, waits for them, and re-layouts  3.34 us
  transfers between devices with their start and end apart: 3, of which 3 were waited for; matrix products, arithmetic and copies ran while one was open for 4% of the time, Pallas kernels for 0%

profile of v4, /device:TPU:1, one launch (start us, length us, event | category | flops | bytes accessed | tf_op | source)
XLA Modules:
  0.0 158.0 jit_solution(15180791018749809666)
XLA Ops:
  0.6 1.5 copy.12
  2.1 11.5 %all-to-all-start = ((s32[128,1,64]{2,1,0:T(1,128)}), s32[128,1,64]{2,1,0:T(1,128)S(1)}, u32[]{:S(2)}, u32[]{:S(2)}) async-start(s32[128,1,64]{2,1,0:T(1,128)} %bitcast.2), calls=%async_computation | async-start | bytes 131072 | tf_op jit(solution)/shard_map/all_to_all | solution.py:538
  13.6 0.8 slice.25
  14.4 1.0 slice.24
  15.4 0.7 fusion.4
  16.2 0.9 copy.17
  17.1 0.0 copy-start.3
  17.1 6.0 %all-to-all-done = s32[128,1,64]{2,1,0:T(1,128)S(1)} async-done(((s32[128,1,64]{2,1,0:T(1,128)}), s32[128,1,64]{2,1,0:T(1,128)S(1)}, u32[]{:S(2)}, u32[]{:S(2)}) %all-to-all-start) | async-done | bytes 32800 | tf_op jit(solution)/shard_map/all_to_all | solution.py:538
  23.0 0.1 copy.13
  23.1 5.1 %shard_map.77 = bf16[4096,128]{1,0:T(8,128)(2,1)} custom-call(s32[64,128]{1,0:T(8,128)S(1)} %bitcast.41, bf16[512,256]{1,0:T(8,128)(2,1)S(1)} %bitcast.40), custom_call_target="tpu_custom_call" | custom-call | tf_op jit(solution)/shard_map/pallas_call | solution.py:475
  28.2 0.0 copy-start
  28.2 0.0 copy-start.1
  28.2 4.6 %all-to-all-start.1 = ((bf16[128,32,128]{2,1,0:T(8,128)(2,1)}), bf16[128,32,128]{2,1,0:T(8,128)(2,1)S(1)}, u32[]{:S(2)}, u32[]{:S(2)}) async-start(bf16[128,32,128]{2,1,0:T(8,128)(2,1)} %bitcast.8), calls=%async_computation.1 | async-start | bytes 2097152 | tf_op jit(solution)/shard_map/all_to_all | solution.py:538
  32.8 0.0 copy-done.3
  32.9 0.2 fusion.3
  33.1 19.0 %all-to-all-done.1 = bf16[128,32,128]{2,1,0:T(8,128)(2,1)S(1)} async-done(((bf16[128,32,128]{2,1,0:T(8,128)(2,1)}), bf16[128,32,128]{2,1,0:T(8,128)(2,1)S(1)}, u32[]{:S(2)}, u32[]{:S(2)}) %all-to-all-start.1) | async-done | bytes 1048608 | tf_op jit(solution)/shard_map/all_to_all | solution.py:538
  52.1 0.0 copy-start.2
  52.1 1.0 copy-done.2
  53.1 0.0 copy-done
  53.1 0.0 copy-done.1
  53.1 42.3 %shard_map.78 = (f32[2,912,128]{2,1,0:T(8,128)S(1)}, f32[4096,128]{1,0:T(8,128)}) custom-call(s32[16]{0:T(128)S(1)} %bitcast.44, s32[17408]{0:T(1024)S(1)} %concatenate.14.lists, f32[2,4]{1,0:T(2,128)S(1)} %bitcast.45, bf16[4096,128]{1,0:T(8,128)(2,1)} %bitcast.46, bf16[2,912,128]{2,1,0:T(8,128)(2,1)S(1)} %pad_maximum_fusion.target, ...), custom_call_target="tpu_custom_call" | custom-call | tf_op jit(solution)/shard_map/pallas_call | solution.py:399
  95.4 25.2 %all-to-all-start.2 = ((f32[128,32,128]{2,1,0:T(8,128)}), f32[128,32,128]{2,1,0:T(8,128)S(1)}, u32[]{:S(2)}, u32[]{:S(2)}) async-start(f32[128,32,128]{2,1,0:T(8,128)} %bitcast.47), calls=%async_computation.2 | async-start | bytes 4194304 | tf_op jit(solution)/shard_map/all_to_all | solution.py:538
  120.5 0.5 broadcast.31
  121.0 0.8 reduce.3
  121.9 0.1 reshape.48.flat
  121.9 0.1 fusion.6
  122.0 1.0 maximum_bitcast_fusion
  123.0 28.0 %all-to-all-done.2 = f32[128,32,128]{2,1,0:T(8,128)S(1)} async-done(((f32[128,32,128]{2,1,0:T(8,128)}), f32[128,32,128]{2,1,0:T(8,128)S(1)}, u32[]{:S(2)}, u32[]{:S(2)}) %all-to-all-start.2) | async-done | bytes 2097184 | tf_op jit(solution)/shard_map/all_to_all | solution.py:538
  151.1 6.9 %shard_map.79 = f32[64,2048]{1,0:T(8,128)} custom-call(s32[64,128]{1,0:T(8,128)S(1)} %bitcast.42, s32[64,128]{1,0:T(8,128)S(1)} %reshape.48.flat, f32[4096,128]{1,0:T(8,128)S(1)} %bitcast.39), custom_call_target="tpu_custom_call" | custom-call | tf_op jit(solution)/shard_map/pallas_call | solution.py:526
  (9 shorter events, 0.2 us)
Async XLA Ops:
  2.1 20.9 %all-to-all-start = ((s32[128,1,64]{2,1,0:T(1,128)}), s32[128,1,64]{2,1,0:T(1,128)S(1)}, u32[]{:S(2)}, u32[]{:S(2)}) async-start(s32[128,1,64]{2,1,0:T(1,128)} %bitcast.2), calls=%async_computation | async-start | bytes 131072 | tf_op jit(solution)/shard_map/all_to_all | solution.py:538
  17.1 15.8 %copy-start.3 = (bf16[1,16,57,256]{3,1,2,0:T(8,128)(2,1)S(1)}, bf16[1,16,57,256]{3,1,2,0:T(8,128)(2,1)}, u32[]{:S(2)}) copy-start(bf16[1,16,57,256]{3,1,2,0:T(8,128)(2,1)} %param.11) | copy-start | bytes 1400836
  28.2 24.9 %copy-start = (s32[1,16]{1,0:T(1,128)S(1)}, s32[1,16]{1,0:T(1,128)}, u32[]{:S(2)}) copy-start(s32[1,16]{1,0:T(1,128)} %param.8) | copy-start | bytes 196
  28.2 24.9 %copy-start.1 = (f32[1,2,4]{2,1,0:T(2,128)S(1)}, f32[1,2,4]{2,1,0:T(2,128)}, u32[]{:S(2)}) copy-start(f32[1,2,4]{2,1,0:T(2,128)} %param.7) | copy-start | bytes 100
  28.2 24.0 %all-to-all-start.1 = ((bf16[128,32,128]{2,1,0:T(8,128)(2,1)}), bf16[128,32,128]{2,1,0:T(8,128)(2,1)S(1)}, u32[]{:S(2)}, u32[]{:S(2)}) async-start(bf16[128,32,128]{2,1,0:T(8,128)(2,1)} %bitcast.8), calls=%async_computation.1 | async-start | bytes 2097152 | tf_op jit(solution)/shard_map/all_to_all | solution.py:538
  52.1 1.0 copy-start.2
  95.4 55.7 %all-to-all-start.2 = ((f32[128,32,128]{2,1,0:T(8,128)}), f32[128,32,128]{2,1,0:T(8,128)S(1)}, u32[]{:S(2)}, u32[]{:S(2)}) async-start(f32[128,32,128]{2,1,0:T(8,128)} %bitcast.47), calls=%async_computation.2 | async-start | bytes 4194304 | tf_op jit(solution)/shard_map/all_to_all | solution.py:538

commit v5 on v4

--- a/solution.py
+++ b/solution.py
@@ -18,6 +18,8 @@
 STEP = 256
 RING = 9
 PAD = 16
+ORDER = "fbfbfbfbfb"
+ONE = ""
 DRIP = 6
 F32 = jnp.float32
 BF16 = jnp.bfloat16
@@ -50,21 +52,24 @@
     lax.fori_loop(0, peers // 8, step, 0)
 
 
-def pack_rows(accs, pairs_ref, peers):
+def pack_rows(accs, pairs_ref, out_ref, sem, peers):
     lane = lax.broadcasted_iota(jnp.int32, (32, LANE), 1)
 
     def step(i, c):
-        for k in range(4):
-            o = i * 4 + k
+        for k in range(8):
+            o = i * 8 + k
             base = pl.multiple_of(o * 64, 64)
             first = sum(acc[pl.ds(base, 32), :] for acc in accs)
             second = sum(acc[pl.ds(pl.multiple_of(base + 32, 32), 32), :] for acc in accs)
             pairs_ref[pl.ds(pl.multiple_of(o * 32, 32), 32), :] = jnp.where(
                 lane < 64, first, pltpu.roll(second, 64, 1)
             )
-        return c
-
-    lax.fori_loop(0, peers // 4, step, 0)
+        part = pl.ds(pl.multiple_of(i * 256, 256), 256)
+        pltpu.make_async_copy(pairs_ref.at[part], out_ref.at[part], sem).start()
+        return c
+
+    lax.fori_loop(0, peers // 8, step, 0)
+    pltpu.make_async_copy(pairs_ref, out_ref, sem).wait()
 
 
 def tiles_kernel(
@@ -75,7 +80,7 @@
     rows, acc0, acc1, acc2, acc3,
     splats, grows, feat_t, geo, weights, ratio, entering_ref, later_ref, pic, tgt, pull_rows, pull_t, grow_t,
     feat_new, geo_new, weights_new, ratio_new, rows_new, cols_new,
-    dy_back, dy_front, qc_front, splats_new,
+    dy_back, dy_front, qc_front, splats_new, packed, sem,
 ):
     accs = (acc0, acc1, acc2, acc3)
     tiles = lens.shape[0]
@@ -167,21 +172,25 @@
         d_weight = dot(pull_t[t], jnp.concatenate([ft, ft], axis=0))
         quads = dot(pull_rows[t], halves)
         quads = quads[:64] + quads[64:]
-        later = jnp.where(keep, later_ref[...], 0.0)
-        sums = [None, None]
+        yield
+        prods, boths, sums = [None, None], [None, None], [None, None]
         for k in (1, 0):
             cut = slice(k * LANE, (k + 1) * LANE)
             weight = (
                 halves[:, 2 * k * LANE:(2 * k + 1) * LANE].astype(F32)
                 + halves[:, (2 * k + 1) * LANE:(2 * k + 2) * LANE].astype(F32)
             )
-            prod = weight * d_weight[:, cut]
-            drip()
-            both = dot(jnp.concatenate(split(prod), axis=1), suffix)
-            drip()
-            h = prod - ratio[slot, :, cut] * (both[:, :LANE] + later)
-            drip()
-            later = later + both[:, LANE:]
+            prods[k] = weight * d_weight[:, cut]
+            drip()
+            boths[k] = dot(jnp.concatenate(split(prods[k]), axis=1), suffix)
+            drip()
+            yield
+        later = jnp.where(keep, later_ref[...], 0.0)
+        for k in (1, 0):
+            cut = slice(k * LANE, (k + 1) * LANE)
+            h = prods[k] - ratio[slot, :, cut] * (boths[k][:, :LANE] + later)
+            drip()
+            later = later + boths[k][:, LANE:]
             drip()
             h = h.reshape(16, 16, LANE)
             dyk = spread(dy_back, cut)
@@ -192,6 +201,7 @@
                 jnp.sum(hy, axis=0),
                 jnp.sum(hy * dyk, axis=0),
             )
+            yield
         later_ref[...] = later
         s0, s1, s2 = (jnp.concatenate([sums[0][j], sums[1][j]], axis=1) for j in range(3))
         sx = s0 * dx
@@ -245,7 +255,7 @@
         dy_front[...] = dy
         qc_front[...] = qc
         entering = jnp.where(keep, entering_ref[...], 0.0)
-        parts = []
+        parts, kept = [], []
         for k in range(2):
             cut = slice(k * LANE, (k + 1) * LANE)
             power = qa[None, :, cut] + qb[None, :, cut] * spread(dy_front, cut) + spread(qc_front, cut)
@@ -255,13 +265,17 @@
             logs = jnp.log2(rest)
             drip()
             both = dot(jnp.concatenate(split(logs), axis=1), prefix)
-            drip()
+            ratio_new[:, cut] = alpha * pl.reciprocal(rest, approx=True)
+            drip()
+            kept.append((alpha, both))
+            yield
+        for alpha, both in kept:
             weight = alpha * jnp.exp2(both[:, :LANE] + entering)
             drip()
             entering = entering + both[:, LANE:]
-            ratio_new[:, cut] = alpha * pl.reciprocal(rest, approx=True)
             parts.extend(split(weight))
             drip()
+            yield
         entering_ref[...] = entering
         halves = jnp.concatenate(parts, axis=1)
         weights_new[...] = halves
@@ -335,13 +349,23 @@
         while moves:
             moves.pop(0)()
 
+    def run(order, front, back):
+        for letter in order:
+            stage = front if letter == "f" else back
+            if stage is not None:
+                next(stage, None)
+        for stage in (front, back):
+            if stage is not None:
+                for _ in stage:
+                    pass
+
     def opening(n, c):
         splats[...] = splats_new[...]
         file(n)
         pull(n - 3)
         prepare(n - 1)
         moves.extend(gather(n))
-        forward(n - 2, drip)
+        run(ONE, forward(n - 2, drip), None)
         flush()
         return c
 
@@ -357,15 +381,14 @@
         pull(n - 3)
         for pair in zip(scatter(n - 8), gather(n)):
             moves.extend(pair)
-        forward(n - 2, drip)
-        backward(n - 7, drip)
+        run(ORDER, forward(n - 2, drip), backward(n - 7, drip))
         flush()
         return c
 
     def closing(n, c):
         turn_back()
         moves.extend(scatter(n - 8))
-        backward(n - 7, drip)
+        run(ONE, None, backward(n - 7, drip))
         flush()
         return c
 
@@ -373,7 +396,7 @@
     lax.fori_loop(7, count + 3, middle, 0)
     file(count + 3)
     lax.fori_loop(count + 3, count + 8, closing, 0)
-    pack_rows(accs, out_pairs, peers)
+    pack_rows(accs, packed, out_pairs, sem, peers)
 
 
 def triangles():
@@ -403,7 +426,7 @@
             jax.ShapeDtypeStruct((peers * 32, LANE), F32),
         ),
         in_specs=[smem] * 3 + [vmem] * 4,
-        out_specs=(vmem, vmem),
+        out_specs=(vmem, pl.BlockSpec(memory_space=pl.ANY)),
         scratch_shapes=[
             *[pltpu.SMEM((steps + 2 * PAD,), jnp.int32)] * 5,
             *[pltpu.VMEM((peers * 64 + 8, LANE), F32)] * (1 + ACCS),
@@ -428,6 +451,8 @@
             pltpu.VMEM((PIX, 2 * ROW), BF16),
             *[pltpu.VMEM((16, STEP), F32)] * 3,
             pltpu.VMEM((STEP, LANE), F32),
+            pltpu.VMEM((peers * 32, LANE), F32),
+            pltpu.SemaphoreType.DMA,
         ],
         compiler_params=pltpu.CompilerParams(vmem_limit_bytes=52 << 20),
     )(lens, flat, cam, pairs, t2, prefix, suffix)

time: 159 us -> 154 us (0.969)
  Pallas kernels: 54.3 us -> 50.2 us
  starting transfers between devices: 41.3 us -> 39.4 us
    pallas_call x1, Pallas kernels: 42.3 us -> 38.2 us  [render(): pl.pallas_call(tiles_kernel, out_shape=(jax.ShapeDtypeStruct((2, FEATS *...]
    all_to_all x3, starting transfers between devices: 41.3 us -> 39.4 us  [exchange(): lax.all_to_all(x, ('gauss', 'view'), split_axis=0, concat_axis=0, tiled=T...]
where the time goes in v5:
time: 154 us; the launch traced here: 152 us
  waiting for transfers between devices  53 us (34%)
  Pallas kernels  50.2 us (33%)
  starting transfers between devices  39.4 us (26%)
  local copies, waits for them, and re-layouts  5.88 us (4%)
  other arithmetic  2.82 us (2%)
    all_to_all x3, waiting for transfers between devices, exchange(): lax.all_to_all(x, ('gauss', 'view'), split_axis=0, concat_axis=0, tiled=T...  53 us
    all_to_all x3, starting transfers between devices, exchange(): lax.all_to_all(x, ('gauss', 'view'), split_axis=0, concat_axis=0, tiled=T...  39.4 us
    pallas_call x1, Pallas kernels, render(): pl.pallas_call(tiles_kernel, out_shape=(jax.ShapeDtypeStruct((2, FEATS *...  38.2 us
    pallas_call x1, Pallas kernels, collect(): pl.pallas_call(collect_kernel, out_shape=jax.ShapeDtypeStruct((ROW, rows)...  6.95 us
    pallas_call x1, Pallas kernels, serve(): pl.pallas_call(serve_kernel, out_shape=jax.ShapeDtypeStruct((peers * 32,...  5.06 us
    unnamed x11, local copies, waits for them, and re-layouts  3.34 us
  transfers between devices with their start and end apart: 3, of which 3 were waited for; matrix products, arithmetic and copies ran while one was open for 4% of the time, Pallas kernels for 0%

profile of v5, /device:TPU:1, one launch (start us, length us, event | category | flops | bytes accessed | tf_op | source)
XLA Modules:
  0.0 152.1 jit_solution(15944987790368780523)
XLA Ops:
  0.6 1.5 copy.12
  2.1 11.5 %all-to-all-start = ((s32[128,1,64]{2,1,0:T(1,128)}), s32[128,1,64]{2,1,0:T(1,128)S(1)}, u32[]{:S(2)}, u32[]{:S(2)}) async-start(s32[128,1,64]{2,1,0:T(1,128)} %bitcast.2), calls=%async_computation | async-start | bytes 131072 | tf_op jit(solution)/shard_map/all_to_all | solution.py:563
  13.6 0.8 slice.25
  14.4 1.0 slice.24
  15.4 0.7 fusion.4
  16.2 0.9 copy.17
  17.1 0.0 copy-start.3
  17.1 6.0 %all-to-all-done = s32[128,1,64]{2,1,0:T(1,128)S(1)} async-done(((s32[128,1,64]{2,1,0:T(1,128)}), s32[128,1,64]{2,1,0:T(1,128)S(1)}, u32[]{:S(2)}, u32[]{:S(2)}) %all-to-all-start) | async-done | bytes 32800 | tf_op jit(solution)/shard_map/all_to_all | solution.py:563
  23.0 0.1 copy.13
  23.1 5.1 %shard_map.77 = bf16[4096,128]{1,0:T(8,128)(2,1)} custom-call(s32[64,128]{1,0:T(8,128)S(1)} %bitcast.41, bf16[512,256]{1,0:T(8,128)(2,1)S(1)} %bitcast.40), custom_call_target="tpu_custom_call" | custom-call | tf_op jit(solution)/shard_map/pallas_call | solution.py:500
  28.2 0.0 copy-start
  28.2 0.0 copy-start.1
  28.2 4.6 %all-to-all-start.1 = ((bf16[128,32,128]{2,1,0:T(8,128)(2,1)}), bf16[128,32,128]{2,1,0:T(8,128)(2,1)S(1)}, u32[]{:S(2)}, u32[]{:S(2)}) async-start(bf16[128,32,128]{2,1,0:T(8,128)(2,1)} %bitcast.8), calls=%async_computation.1 | async-start | bytes 2097152 | tf_op jit(solution)/shard_map/all_to_all | solution.py:563
  32.8 0.0 copy-done.3
  32.9 0.2 fusion.3
  33.1 19.0 %all-to-all-done.1 = bf16[128,32,128]{2,1,0:T(8,128)(2,1)S(1)} async-done(((bf16[128,32,128]{2,1,0:T(8,128)(2,1)}), bf16[128,32,128]{2,1,0:T(8,128)(2,1)S(1)}, u32[]{:S(2)}, u32[]{:S(2)}) %all-to-all-start.1) | async-done | bytes 1048608 | tf_op jit(solution)/shard_map/all_to_all | solution.py:563
  52.1 0.0 copy-start.2
  52.1 1.0 copy-done.2
  53.1 0.0 copy-done
  53.1 0.0 copy-done.1
  53.1 38.2 %shard_map.78 = (f32[2,912,128]{2,1,0:T(8,128)S(1)}, f32[4096,128]{1,0:T(8,128)}) custom-call(s32[16]{0:T(128)S(1)} %bitcast.44, s32[17408]{0:T(1024)S(1)} %concatenate.14.lists, f32[2,4]{1,0:T(2,128)S(1)} %bitcast.45, bf16[4096,128]{1,0:T(8,128)(2,1)} %bitcast.46, bf16[2,912,128]{2,1,0:T(8,128)(2,1)S(1)} %pad_maximum_fusion.target, ...), custom_call_target="tpu_custom_call" | custom-call | tf_op jit(solution)/shard_map/pallas_call | solution.py:422
  91.3 23.3 %all-to-all-start.2 = ((f32[128,32,128]{2,1,0:T(8,128)}), f32[128,32,128]{2,1,0:T(8,128)S(1)}, u32[]{:S(2)}, u32[]{:S(2)}) async-start(f32[128,32,128]{2,1,0:T(8,128)} %bitcast.47), calls=%async_computation.2 | async-start | bytes 4194304 | tf_op jit(solution)/shard_map/all_to_all | solution.py:563
  114.6 0.5 broadcast.31
  115.1 0.8 reduce.3
  115.9 0.1 reshape.48.flat
  116.0 0.1 fusion.6
  116.1 1.0 maximum_bitcast_fusion
  117.1 28.0 %all-to-all-done.2 = f32[128,32,128]{2,1,0:T(8,128)S(1)} async-done(((f32[128,32,128]{2,1,0:T(8,128)}), f32[128,32,128]{2,1,0:T(8,128)S(1)}, u32[]{:S(2)}, u32[]{:S(2)}) %all-to-all-start.2) | async-done | bytes 2097184 | tf_op jit(solution)/shard_map/all_to_all | solution.py:563
  145.1 6.9 %shard_map.79 = f32[64,2048]{1,0:T(8,128)} custom-call(s32[64,128]{1,0:T(8,128)S(1)} %bitcast.42, s32[64,128]{1,0:T(8,128)S(1)} %reshape.48.flat, f32[4096,128]{1,0:T(8,128)S(1)} %bitcast.39), custom_call_target="tpu_custom_call" | custom-call | tf_op jit(solution)/shard_map/pallas_call | solution.py:551
  (9 shorter events, 0.2 us)
Async XLA Ops:
  2.1 20.9 %all-to-all-start = ((s32[128,1,64]{2,1,0:T(1,128)}), s32[128,1,64]{2,1,0:T(1,128)S(1)}, u32[]{:S(2)}, u32[]{:S(2)}) async-start(s32[128,1,64]{2,1,0:T(1,128)} %bitcast.2), calls=%async_computation | async-start | bytes 131072 | tf_op jit(solution)/shard_map/all_to_all | solution.py:563
  17.1 15.8 %copy-start.3 = (bf16[1,16,57,256]{3,1,2,0:T(8,128)(2,1)S(1)}, bf16[1,16,57,256]{3,1,2,0:T(8,128)(2,1)}, u32[]{:S(2)}) copy-start(bf16[1,16,57,256]{3,1,2,0:T(8,128)(2,1)} %param.11) | copy-start | bytes 1400836
  28.2 24.9 %copy-start = (s32[1,16]{1,0:T(1,128)S(1)}, s32[1,16]{1,0:T(1,128)}, u32[]{:S(2)}) copy-start(s32[1,16]{1,0:T(1,128)} %param.8) | copy-start | bytes 196
  28.2 24.9 %copy-start.1 = (f32[1,2,4]{2,1,0:T(2,128)S(1)}, f32[1,2,4]{2,1,0:T(2,128)}, u32[]{:S(2)}) copy-start(f32[1,2,4]{2,1,0:T(2,128)} %param.7) | copy-start | bytes 100
  28.2 24.0 %all-to-all-start.1 = ((bf16[128,32,128]{2,1,0:T(8,128)(2,1)}), bf16[128,32,128]{2,1,0:T(8,128)(2,1)S(1)}, u32[]{:S(2)}, u32[]{:S(2)}) async-start(bf16[128,32,128]{2,1,0:T(8,128)(2,1)} %bitcast.8), calls=%async_computation.1 | async-start | bytes 2097152 | tf_op jit(solution)/shard_map/all_to_all | solution.py:563
  52.1 1.0 copy-start.2
  91.3 53.9 %all-to-all-start.2 = ((f32[128,32,128]{2,1,0:T(8,128)}), f32[128,32,128]{2,1,0:T(8,128)S(1)}, u32[]{:S(2)}, u32[]{:S(2)}) async-start(f32[128,32,128]{2,1,0:T(8,128)} %bitcast.47), calls=%async_computation.2 | async-start | bytes 4194304 | tf_op jit(solution)/shard_map/all_to_all | solution.py:563

commit v6 on v5

--- a/solution.py
+++ b/solution.py
@@ -18,7 +18,7 @@
 STEP = 256
 RING = 9
 PAD = 16
-ORDER = "fbfbfbfbfb"
+ORDER = "fbfbfbffbb"
 ONE = ""
 DRIP = 6
 F32 = jnp.float32
@@ -392,10 +392,19 @@
         flush()
         return c
 
-    lax.fori_loop(0, 7, opening, 0)
+    moves.extend(gather(0))
+    flush()
+    splats[...] = splats_new[...]
+    prepare(0)
+    moves.extend(gather(1))
+    flush()
+    lax.fori_loop(2, 7, opening, 0)
     lax.fori_loop(7, count + 3, middle, 0)
     file(count + 3)
-    lax.fori_loop(count + 3, count + 8, closing, 0)
+    lax.fori_loop(count + 3, count + 7, closing, 0)
+    turn_back()
+    moves.extend(scatter(count - 1))
+    flush()
     pack_rows(accs, packed, out_pairs, sem, peers)
 
 
@@ -454,7 +463,7 @@
             pltpu.VMEM((peers * 32, LANE), F32),
             pltpu.SemaphoreType.DMA,
         ],
-        compiler_params=pltpu.CompilerParams(vmem_limit_bytes=52 << 20),
+        compiler_params=pltpu.CompilerParams(vmem_limit_bytes=202 << 18),
     )(lens, flat, cam, pairs, t2, prefix, suffix)
     image = jnp.concatenate([image[0], image[1]], axis=1).reshape(FEATS, tiles, PIX)
     return jnp.transpose(image, (1, 0, 2)), grads

time: 154 us -> 152 us (0.987); the launches traced: 152 us -> 152 us
  starting transfers between devices: 39.4 us -> 41.3 us
    all_to_all x3, starting transfers between devices: 39.4 us -> 41.3 us  [exchange(): lax.all_to_all(x, ('gauss', 'view'), split_axis=0, concat_axis=0, tiled=T...]
    unnamed x11 -> x9, local copies, waits for them, and re-layouts: 3.34 us -> 2.37 us
where the time goes in v6:
time: 152 us
  waiting for transfers between devices  53 us (35%)
  Pallas kernels  49.6 us (33%)
  starting transfers between devices  41.3 us (27%)
  local copies, waits for them, and re-layouts  4.91 us (3%)
  other arithmetic  2.82 us (2%)
    all_to_all x3, waiting for transfers between devices, exchange(): lax.all_to_all(x, ('gauss', 'view'), split_axis=0, concat_axis=0, tiled=T...  53 us
    all_to_all x3, starting transfers between devices, exchange(): lax.all_to_all(x, ('gauss', 'view'), split_axis=0, concat_axis=0, tiled=T...  41.3 us
    pallas_call x1, Pallas kernels, render(): pl.pallas_call(tiles_kernel, out_shape=(jax.ShapeDtypeStruct((2, FEATS *...  37.6 us
    pallas_call x1, Pallas kernels, collect(): pl.pallas_call(collect_kernel, out_shape=jax.ShapeDtypeStruct((ROW, rows)...  6.95 us
    pallas_call x1, Pallas kernels, serve(): pl.pallas_call(serve_kernel, out_shape=jax.ShapeDtypeStruct((peers * 32,...  5.06 us
  transfers between devices with their start and end apart: 3, of which 3 were waited for; matrix products, arithmetic and copies ran while one was open for 4% of the time, Pallas kernels for 0%

profile of v6, /device:TPU:1, one launch (start us, length us, event | category | flops | bytes accessed | tf_op | source)
XLA Modules:
  0.0 152.5 jit_solution(13967710740204460050)
XLA Ops:
  0.6 1.5 copy.12
  2.1 11.5 %all-to-all-start = ((s32[128,1,64]{2,1,0:T(1,128)}), s32[128,1,64]{2,1,0:T(1,128)S(1)}, u32[]{:S(2)}, u32[]{:S(2)}) async-start(s32[128,1,64]{2,1,0:T(1,128)} %bitcast.2), calls=%async_computation | async-start | bytes 131072 | tf_op jit(solution)/shard_map/all_to_all | solution.py:572
  13.6 0.8 slice.25
  14.4 1.0 slice.24
  15.4 0.7 fusion.4
  16.2 0.9 copy.17
  17.1 0.0 copy-start.2
  17.1 6.0 %all-to-all-done = s32[128,1,64]{2,1,0:T(1,128)S(1)} async-done(((s32[128,1,64]{2,1,0:T(1,128)}), s32[128,1,64]{2,1,0:T(1,128)S(1)}, u32[]{:S(2)}, u32[]{:S(2)}) %all-to-all-start) | async-done | bytes 32800 | tf_op jit(solution)/shard_map/all_to_all | solution.py:572
  23.0 0.1 copy.13
  23.1 5.1 %shard_map.77 = bf16[4096,128]{1,0:T(8,128)(2,1)} custom-call(s32[64,128]{1,0:T(8,128)S(1)} %bitcast.42, bf16[512,256]{1,0:T(8,128)(2,1)S(1)} %bitcast.41), custom_call_target="tpu_custom_call" | custom-call | tf_op jit(solution)/shard_map/pallas_call | solution.py:509
  28.2 0.0 copy-start
  28.2 0.0 copy-start.1
  28.2 4.6 %all-to-all-start.1 = ((bf16[128,32,128]{2,1,0:T(8,128)(2,1)}), bf16[128,32,128]{2,1,0:T(8,128)(2,1)S(1)}, u32[]{:S(2)}, u32[]{:S(2)}) async-start(bf16[128,32,128]{2,1,0:T(8,128)(2,1)} %bitcast.8), calls=%async_computation.1 | async-start | bytes 2097152 | tf_op jit(solution)/shard_map/all_to_all | solution.py:572
  32.8 0.0 copy-done.2
  32.9 0.2 fusion.3
  33.1 19.0 %all-to-all-done.1 = bf16[128,32,128]{2,1,0:T(8,128)(2,1)S(1)} async-done(((bf16[128,32,128]{2,1,0:T(8,128)(2,1)}), bf16[128,32,128]{2,1,0:T(8,128)(2,1)S(1)}, u32[]{:S(2)}, u32[]{:S(2)}) %all-to-all-start.1) | async-done | bytes 1048608 | tf_op jit(solution)/shard_map/all_to_all | solution.py:572
  52.1 0.0 copy-done
  52.1 0.0 copy-done.1
  52.1 37.6 %shard_map.78 = (f32[2,912,128]{2,1,0:T(8,128)S(1)}, f32[4096,128]{1,0:T(8,128)}) custom-call(s32[16]{0:T(128)S(1)} %bitcast.45, s32[17408]{0:T(1024)S(1)} %concatenate.14.lists, f32[2,4]{1,0:T(2,128)S(1)} %bitcast.46, bf16[4096,128]{1,0:T(8,128)(2,1)S(1)} %bitcast.40, bf16[2,912,128]{2,1,0:T(8,128)(2,1)S(1)} %pad_maximum_fusion.target, ...), custom_call_target="tpu_custom_call" | custom-call | tf_op jit(solution)/shard_map/pallas_call | solution.py:431
  89.8 25.2 %all-to-all-start.2 = ((f32[128,32,128]{2,1,0:T(8,128)}), f32[128,32,128]{2,1,0:T(8,128)S(1)}, u32[]{:S(2)}, u32[]{:S(2)}) async-start(f32[128,32,128]{2,1,0:T(8,128)} %bitcast.47), calls=%async_computation.2 | async-start | bytes 4194304 | tf_op jit(solution)/shard_map/all_to_all | solution.py:572
  115.0 0.5 broadcast.31
  115.5 0.8 reduce.3
  116.3 0.1 reshape.48.flat
  116.4 0.1 fusion.6
  116.4 1.0 maximum_bitcast_fusion
  117.5 28.0 %all-to-all-done.2 = f32[128,32,128]{2,1,0:T(8,128)S(1)} async-done(((f32[128,32,128]{2,1,0:T(8,128)}), f32[128,32,128]{2,1,0:T(8,128)S(1)}, u32[]{:S(2)}, u32[]{:S(2)}) %all-to-all-start.2) | async-done | bytes 2097184 | tf_op jit(solution)/shard_map/all_to_all | solution.py:572
  145.5 7.0 %shard_map.79 = f32[64,2048]{1,0:T(8,128)} custom-call(s32[64,128]{1,0:T(8,128)S(1)} %bitcast.43, s32[64,128]{1,0:T(8,128)S(1)} %reshape.48.flat, f32[4096,128]{1,0:T(8,128)S(1)} %bitcast.39), custom_call_target="tpu_custom_call" | custom-call | tf_op jit(solution)/shard_map/pallas_call | solution.py:560
  (9 shorter events, 0.2 us)
Async XLA Ops:
  2.1 20.9 %all-to-all-start = ((s32[128,1,64]{2,1,0:T(1,128)}), s32[128,1,64]{2,1,0:T(1,128)S(1)}, u32[]{:S(2)}, u32[]{:S(2)}) async-start(s32[128,1,64]{2,1,0:T(1,128)} %bitcast.2), calls=%async_computation | async-start | bytes 131072 | tf_op jit(solution)/shard_map/all_to_all | solution.py:572
  17.1 15.8 %copy-start.2 = (bf16[1,16,57,256]{3,1,2,0:T(8,128)(2,1)S(1)}, bf16[1,16,57,256]{3,1,2,0:T(8,128)(2,1)}, u32[]{:S(2)}) copy-start(bf16[1,16,57,256]{3,1,2,0:T(8,128)(2,1)} %param.11) | copy-start | bytes 1400836
  28.2 24.0 %copy-start = (s32[1,16]{1,0:T(1,128)S(1)}, s32[1,16]{1,0:T(1,128)}, u32[]{:S(2)}) copy-start(s32[1,16]{1,0:T(1,128)} %param.8) | copy-start | bytes 196
  28.2 24.0 %copy-start.1 = (f32[1,2,4]{2,1,0:T(2,128)S(1)}, f32[1,2,4]{2,1,0:T(2,128)}, u32[]{:S(2)}) copy-start(f32[1,2,4]{2,1,0:T(2,128)} %param.7) | copy-start | bytes 100
  28.2 24.0 %all-to-all-start.1 = ((bf16[128,32,128]{2,1,0:T(8,128)(2,1)}), bf16[128,32,128]{2,1,0:T(8,128)(2,1)S(1)}, u32[]{:S(2)}, u32[]{:S(2)}) async-start(bf16[128,32,128]{2,1,0:T(8,128)(2,1)} %bitcast.8), calls=%async_computation.1 | async-start | bytes 2097152 | tf_op jit(solution)/shard_map/all_to_all | solution.py:572
  89.8 55.7 %all-to-all-start.2 = ((f32[128,32,128]{2,1,0:T(8,128)}), f32[128,32,128]{2,1,0:T(8,128)S(1)}, u32[]{:S(2)}, u32[]{:S(2)}) async-start(f32[128,32,128]{2,1,0:T(8,128)} %bitcast.47), calls=%async_computation.2 | async-start | bytes 4194304 | tf_op jit(solution)/shard_map/all_to_all | solution.py:572
